TPU v7x, 256 devices: a whole 4x4x8 slice. The times are simulated.
256 devices in a mesh: section: 2 (over core), dp: 8 (over x, y_hi), tensor: 16 (over y_lo, z).
Axes of the slice: x: 4, y: 4 (y_hi: 2, y_lo: 2; y = y_hi * 2 + y_lo), z: 8, core: 2. Of those that a mesh axis runs over, the one named last changes fastest.
Arguments:
- inputs: bfloat16 [2, 128, 8192], P(None, 'dp', 'tensor'), may hold values from -6 to 6
- cotangent: bfloat16 [2, 128, 8192], P(None, 'dp', 'tensor'), may hold values from -6 to 6
- scale_exps: int32 [2, 16, 64], P(None, 'dp', 'tensor'), may hold values from -9 to -6
- up_weight: bfloat16 [2, 8192, 20480], P('section', 'tensor', 'dp'), may hold values from -0.0625 to 0.0625
- down_weight: bfloat16 [2, 20480, 8192], P('section', 'dp', 'tensor'), may hold values from -0.0390625 to 0.0390625
Outputs:
- section_out: bfloat16 [2, 2, 128, 8192], P('section', None, 'dp', 'tensor')
- input_grads: bfloat16 [2, 2, 128, 8192], P('section', None, 'dp', 'tensor')
- up_grads: bfloat16 [2, 8192, 20480], P('section', 'tensor', 'dp')
- down_grads: bfloat16 [2, 20480, 8192], P('section', 'dp', 'tensor')
All inputs are finite; a program needn't handle non-finite values.
Results may differ from a plain program's by a relative error of at most 0.039.
Values may be sent and summed in bfloat16 or wider, within the bound.
A program may use at most 128 MiB of HBM per device.

v0:
```python
import math

import jax
import jax.numpy as jnp
from jax import lax
from jax.sharding import PartitionSpec as P

gelu_coef = math.sqrt(2.0 / math.pi)


def passed_along(array, axis, by):
    devices = lax.axis_size(axis)
    pairs = [(i, i + by) for i in range(devices) if 0 <= i + by < devices]
    return lax.ppermute(array, axis, pairs)


def gelu_value(values):
    inner_arg = gelu_coef * (values + 0.044715 * values * values * values)
    return 0.5 * values * (1.0 + jnp.tanh(inner_arg))


def gelu_slope(values):
    tangent = jnp.tanh(gelu_coef * (values + 0.044715 * values * values * values))
    return 0.5 * (1.0 + tangent) + 0.5 * values * (1.0 - tangent * tangent) * gelu_coef * (
        1.0 + 3.0 * 0.044715 * values * values
    )


def round_trip(values):
    return lax.optimization_barrier(values.astype(jnp.bfloat16)).astype(jnp.float32)


def tile_factor(exponents, row_total, col_total, sign_value):
    row_tiles, col_tiles = exponents.shape
    factor = jnp.exp2(sign_value * exponents.astype(jnp.float32))
    spread_out = jnp.broadcast_to(
        factor[:, None, :, None],
        (row_tiles, row_total // row_tiles, col_tiles, col_total // col_tiles),
    )
    return spread_out.reshape(row_total, col_total)


def per_device(inputs, cotangent, scale_exps, up_weight, down_weight):
    section_index = lax.axis_index("section")
    is_first = section_index == 0
    micro_count = inputs.shape[0]
    local_rows = inputs.shape[1]
    local_cols = inputs.shape[2]
    w_up = up_weight[0]
    w_down = down_weight[0]
    zero_rows = jnp.zeros_like(inputs[0])
    carried = zero_rows
    stash_list = []
    forward_list = []
    for tick_index in range(micro_count + 1):
        fresh_rows = inputs[tick_index] if tick_index < micro_count else zero_rows
        tok_rows = jnp.where(is_first, fresh_rows, carried)
        gathered = lax.all_gather(tok_rows, "dp", axis=0, tiled=True)
        partial_value = round_trip(jnp.dot(gathered, w_up, preferred_element_type=jnp.float32))
        hidden = lax.psum(partial_value.astype(jnp.bfloat16), "tensor").astype(jnp.float32)
        active = gelu_value(hidden).astype(jnp.bfloat16)

        def out_term(start_row, row_count, active=active):
            return jnp.dot(active, w_down, preferred_element_type=jnp.float32)

        mixed_rows = lax.psum_scatter(
            out_term(jnp.int32(0), local_rows * lax.axis_size("dp")).astype(jnp.bfloat16),
            "dp",
            scatter_dimension=0,
            tiled=True,
        ).astype(jnp.float32)
        result = (tok_rows.astype(jnp.float32) + mixed_rows).astype(jnp.bfloat16)
        forward_list.append(result)
        if tick_index < micro_count:
            carried = passed_along(result, "section", 1)
        stash_list.append((gathered, hidden, active))
    up_total = jnp.zeros(w_up.shape, jnp.float32)
    down_total = jnp.zeros(w_down.shape, jnp.float32)
    incoming = zero_rows
    grad_list = []
    for tick_index in range(micro_count + 1):
        quant_index = max(micro_count - 1 - tick_index, 0)
        restore_index = min(micro_count - tick_index, micro_count - 1)
        target_rows = (
            cotangent[micro_count - 1 - tick_index] if tick_index < micro_count else zero_rows
        )
        restore_factor = tile_factor(scale_exps[restore_index], local_rows, local_cols, 1.0)
        restored = (incoming.astype(jnp.float32) * restore_factor).astype(jnp.bfloat16)
        grad_rows = jnp.where(is_first, restored, target_rows)
        gathered, hidden, active = stash_list[micro_count - tick_index]
        grads_full = lax.all_gather(grad_rows, "dp", axis=0, tiled=True)
        back_term = round_trip(
            jnp.einsum("td,fd->tf", grads_full, w_down, preferred_element_type=jnp.float32)
        )
        back_sum = lax.psum(back_term.astype(jnp.bfloat16), "tensor").astype(jnp.float32)
        delta_local = (back_sum * gelu_slope(hidden)).astype(jnp.bfloat16)
        down_total = down_total + jnp.einsum(
            "tf,td->fd", active, grads_full, preferred_element_type=jnp.float32
        )
        up_total = up_total + jnp.einsum(
            "td,tf->df", gathered, delta_local, preferred_element_type=jnp.float32
        )

        def in_term(start_row, row_count, delta_local=delta_local):
            return jnp.einsum("tf,df->td", delta_local, w_up, preferred_element_type=jnp.float32)

        spread = lax.psum_scatter(
            in_term(jnp.int32(0), local_rows * lax.axis_size("dp")).astype(jnp.bfloat16),
            "dp",
            scatter_dimension=0,
            tiled=True,
        ).astype(jnp.float32)
        through = grad_rows.astype(jnp.float32) + spread
        grad_list.append(through.astype(jnp.bfloat16))
        if tick_index < micro_count:
            quant_factor = tile_factor(scale_exps[quant_index], local_rows, local_cols, -1.0)
            packed = jnp.clip(through * quant_factor, -448.0, 448.0).astype(jnp.bfloat16)
            incoming = passed_along(packed, "section", -1)
    forward_stack = jnp.stack(forward_list)
    section_out = lax.dynamic_slice_in_dim(forward_stack, section_index, micro_count, 0)
    grad_stack = jnp.stack(grad_list[::-1])
    input_grads = lax.dynamic_slice_in_dim(grad_stack, section_index, micro_count, 0)
    return (
        section_out[None],
        input_grads[None],
        up_total.astype(jnp.bfloat16)[None],
        down_total.astype(jnp.bfloat16)[None],
    )


def solution(mesh):
    in_specs = (
        P(None, "dp", "tensor"),
        P(None, "dp", "tensor"),
        P(None, "dp", "tensor"),
        P("section", "tensor", "dp"),
        P("section", "dp", "tensor"),
    )
    out_specs = (
        P("section", None, "dp", "tensor"),
        P("section", None, "dp", "tensor"),
        P("section", "tensor", "dp"),
        P("section", "dp", "tensor"),
    )
    return jax.shard_map(
        per_device, mesh=mesh, in_specs=in_specs, out_specs=out_specs, check_vma=False
    )
```

profile of v0, /device:TPU:2, one launch (start us, length us, event | category | flops | bytes accessed | tf_op | source)
XLA Modules:
  0.0 1362.8 jit_solution(2945059377948378345)
XLA Ops:
  7.2 0.9 slice_select_fusion
  8.1 33.8 %all-gather = bf16[1,128,512]{2,1,0:T(8,128)(2,1)S(1)} all-gather(bf16[1,16,512]{2,1,0:T(8,128)(2,1)S(1)} %slice_select_fusion), channel_id=2, replica_groups=mesh['section'=2,'dp'=8,'tensor'=16] {'dp'}, dimensions={1}, use_global_device_ids=true | all-gather | bytes 147456 | tf_op jit(solution)/shard_map/all_gather | solution.py:58
  41.9 3.1 convolution_convert_fusion.5
  45.1 139.3 %all-reduce.7.cloned.1.call-done = bf16[128,2560]{1,0:T(8,128)(2,1)} async-done(((bf16[128,2560]{1,0:T(8,128)(2,1)}), bf16[128,2560]{1,0:T(8,128)(2,1)}) %all-reduce.7.cloned.1.call-update) | async-done | bytes 655376 | tf_op jit(solution)/shard_map/psum | solution.py:60
  184.3 2.4 fusion.62
  186.8 74.3 %reduce-scatter.7.cloned.1.call-done = bf16[16,512]{1,0:T(8,128)(2,1)} async-done(((bf16[128,512]{1,0:T(8,128)(2,1)}), bf16[16,512]{1,0:T(8,128)(2,1)}) %reduce-scatter.7.cloned.1.call-update) | async-done | bytes 16400 | tf_op jit(solution)/shard_map/reduce_scatter | solution.py:66
  261.1 0.7 fusion.82
  261.8 1.3 collective-permute-start
  263.1 0.8 collective-permute-done
  263.9 32.4 %all_gather.19 = bf16[128,512]{1,0:T(8,128)(2,1)S(1)} all-gather(bf16[16,512]{1,0:T(8,128)(2,1)S(1)} %bitcast_select_fusion), channel_id=1, replica_groups=mesh['section'=2,'dp'=8,'tensor'=16] {'dp'}, dimensions={0}, use_global_device_ids=true | all-gather | bytes 147456 | tf_op jit(solution)/shard_map/all_gather | solution.py:58
  296.3 3.1 convolution_convert_fusion.4
  300.1 136.6 %all-reduce.9.cloned.1.call-done = bf16[128,2560]{1,0:T(8,128)(2,1)} async-done(((bf16[128,2560]{1,0:T(8,128)(2,1)}), bf16[128,2560]{1,0:T(8,128)(2,1)}) %all-reduce.9.cloned.1.call-update) | async-done | bytes 655376 | tf_op jit(solution)/shard_map/psum | solution.py:60
  436.7 2.4 fusion.65
  439.3 32.1 %all_gather.21 = bf16[128,512]{1,0:T(8,128)(2,1)S(1)} all-gather(bf16[16,512]{1,0:T(8,128)(2,1)S(1)} %fusion.96), channel_id=1, replica_groups=mesh['section'=2,'dp'=8,'tensor'=16] {'dp'}, dimensions={0}, use_global_device_ids=true | all-gather | bytes 147456 | tf_op jit(solution)/shard_map/all_gather | solution.py:91
  471.4 41.5 %reduce-scatter.9.cloned.1.call-done = bf16[16,512]{1,0:T(8,128)(2,1)} async-done(((bf16[128,512]{1,0:T(8,128)(2,1)}), bf16[16,512]{1,0:T(8,128)(2,1)}) %reduce-scatter.9.cloned.1.call-update) | async-done | bytes 16400 | tf_op jit(solution)/shard_map/reduce_scatter | solution.py:66
  512.9 0.7 add_convert_fusion.4
  513.7 1.4 collective-permute-start.1
  515.1 1.8 convolution_convert_fusion.2
  516.9 32.4 %all_gather.20 = bf16[128,512]{1,0:T(8,128)(2,1)S(1)} all-gather(bf16[16,512]{1,0:T(8,128)(2,1)S(1)} %broadcast_select_fusion), channel_id=1, replica_groups=mesh['section'=2,'dp'=8,'tensor'=16] {'dp'}, dimensions={0}, use_global_device_ids=true | all-gather | bytes 147456 | tf_op jit(solution)/shard_map/all_gather | solution.py:58
  550.0 1.4 convolution_convert_fusion.3
  551.5 140.1 %all-reduce.15.cloned.1.call-done = (bf16[128,2560]{1,0:T(8,128)(2,1)}, bf16[128,2560]{1,0:T(8,128)(2,1)}) async-done(((bf16[128,2560]{1,0:T(8,128)(2,1)}, bf16[128,2560]{1,0:T(8,128)(2,1)}), (bf16[128,2560]{1,0:T(8,128)(2,1)}, bf16[128,2560]{1,0:T(8,128)(2,1)})) %all-reduce.15.cloned.1.call-update) | async-done | bytes 1310736 | tf_op jit(solution)/shard_map/psum | solution.py:60
  691.5 3.9 fusion.53
  695.5 72.2 %reduce-scatter.13.cloned.1.call-done = bf16[16,512]{1,0:T(8,128)(2,1)} async-done(((bf16[128,512]{1,0:T(8,128)(2,1)}), bf16[16,512]{1,0:T(8,128)(2,1)}) %reduce-scatter.13.cloned.1.call-update) | async-done | bytes 16400 | tf_op jit(solution)/shard_map/reduce_scatter | solution.py:107
  767.7 1.3 fusion.91
  769.0 1.3 collective-permute-start.2
  770.3 1.8 collective-permute-done.2
  772.1 32.4 %all_gather.22 = bf16[128,512]{1,0:T(8,128)(2,1)S(1)} all-gather(bf16[16,512]{1,0:T(8,128)(2,1)S(1)} %fusion.95), channel_id=1, replica_groups=mesh['section'=2,'dp'=8,'tensor'=16] {'dp'}, dimensions={0}, use_global_device_ids=true | all-gather | bytes 147456 | tf_op jit(solution)/shard_map/all_gather | solution.py:91
  805.2 1.8 convolution_convert_fusion.1
  807.1 1.3 fusion.68
  808.4 4.4 fusion.102
  812.9 131.5 %all-reduce.11.cloned.1.call-done = bf16[128,2560]{1,0:T(8,128)(2,1)} async-done(((bf16[128,2560]{1,0:T(8,128)(2,1)}), bf16[128,2560]{1,0:T(8,128)(2,1)}) %all-reduce.11.cloned.1.call-update) | async-done | bytes 655376 | tf_op jit(solution)/shard_map/psum | solution.py:95
  944.4 3.7 fusion.56
  948.2 73.0 %reduce-scatter.11.cloned.1.call-done = bf16[16,512]{1,0:T(8,128)(2,1)} async-done(((bf16[128,512]{1,0:T(8,128)(2,1)}), bf16[16,512]{1,0:T(8,128)(2,1)}) %reduce-scatter.11.cloned.1.call-update) | async-done | bytes 16400 | tf_op jit(solution)/shard_map/reduce_scatter | solution.py:66
  1021.1 0.7 fusion.92
  1021.9 1.4 fusion.81
  1023.3 76.7 %reduce-scatter.15.cloned.1.call-done = bf16[16,512]{1,0:T(8,128)(2,1)} async-done(((bf16[128,512]{1,0:T(8,128)(2,1)}), bf16[16,512]{1,0:T(8,128)(2,1)}) %reduce-scatter.15.cloned.1.call-update) | async-done | bytes 16400 | tf_op jit(solution)/shard_map/reduce_scatter | solution.py:107
  1100.0 1.3 fusion.90
  1101.3 1.4 collective-permute-start.3
  1102.7 4.1 fusion.99
  1106.9 32.4 %all_gather.23 = bf16[128,512]{1,0:T(8,128)(2,1)S(1)} all-gather(bf16[16,512]{1,0:T(8,128)(2,1)S(1)} %fusion.94), channel_id=1, replica_groups=mesh['section'=2,'dp'=8,'tensor'=16] {'dp'}, dimensions={0}, use_global_device_ids=true | all-gather | bytes 147456 | tf_op jit(solution)/shard_map/all_gather | solution.py:91
  1140.0 1.8 convolution_convert_fusion
  1142.0 4.8 fusion.107
  1146.9 6.8 fusion.1
  1153.7 125.4 %all-reduce.13.cloned.1.call-done = bf16[128,2560]{1,0:T(8,128)(2,1)} async-done(((bf16[128,2560]{1,0:T(8,128)(2,1)}), bf16[128,2560]{1,0:T(8,128)(2,1)}) %all-reduce.13.cloned.1.call-update) | async-done | bytes 655376 | tf_op jit(solution)/shard_map/psum | solution.py:95
  1279.1 3.7 fusion.59
  1282.9 2.5 fusion.71
  1285.4 5.9 fusion
  1291.4 63.5 %reduce-scatter.17.cloned.1.call-done = bf16[16,512]{1,0:T(8,128)(2,1)} async-done(((bf16[128,512]{1,0:T(8,128)(2,1)}), bf16[16,512]{1,0:T(8,128)(2,1)}) %reduce-scatter.17.cloned.1.call-update) | async-done | bytes 16400 | tf_op jit(solution)/shard_map/reduce_scatter | solution.py:107
  (78 shorter events, 5.1 us)
Async XLA Ops:
  7.2 177.2 %copy-start = (bf16[1,2560,512]{2,1,0:T(8,128)(2,1)S(1)}, bf16[1,2560,512]{2,1,0:T(8,128)(2,1)}, u32[]{:S(2)}) copy-start(bf16[1,2560,512]{2,1,0:T(8,128)(2,1)} %param.9) | copy-start | bytes 7864324
  7.2 177.2 %all-reduce.7.cloned.1.call-start = ((), (), s32[]{:S(2)}) async-start(), calls=%async_computation.6 | async-start | bytes 1310720 | tf_op jit(solution)/shard_map/psum | solution.py:60
  45.0 216.1 %copy-start.14 = (bf16[2,16,512]{2,1,0:T(8,128)(2,1)S(1)}, bf16[2,16,512]{2,1,0:T(8,128)(2,1)}, u32[]{:S(2)}) copy-start(bf16[2,16,512]{2,1,0:T(8,128)(2,1)} %param.5) | copy-start | bytes 98308
  45.0 216.1 %reduce-scatter.7.cloned.1.call-start = ((), (), s32[]{:S(2)}) async-start(), calls=%async_computation.7 | async-start | bytes 147456 | tf_op jit(solution)/shard_map/reduce_scatter | solution.py:66
  186.7 250.0 %all-reduce.9.cloned.1.call-start = ((), (), s32[]{:S(2)}) async-start(), calls=%async_computation.8 | async-start | bytes 1310720 | tf_op jit(solution)/shard_map/psum | solution.py:60
  261.8 37.6 %copy-start.15 = (bf16[16,512]{1,0:T(8,128)(2,1)}, bf16[16,512]{1,0:T(8,128)(2,1)S(1)}, u32[]{:S(2)}) copy-start(bf16[16,512]{1,0:T(8,128)(2,1)S(1)} %fusion.82) | copy-start | bytes 49156
  261.8 2.1 collective-permute-start
  296.3 3.2 copy-start.22
  299.5 213.5 %reduce-scatter.9.cloned.1.call-start = ((), (), s32[]{:S(2)}) async-start(), calls=%async_computation.9 | async-start | bytes 147456 | tf_op jit(solution)/shard_map/reduce_scatter | solution.py:66
  300.1 139.1 %copy-start.20 = (bf16[2,16,512]{2,1,0:T(8,128)(2,1)S(1)}, bf16[2,16,512]{2,1,0:T(8,128)(2,1)}, u32[]{:S(2)}) copy-start(bf16[2,16,512]{2,1,0:T(8,128)(2,1)} %param.6) | copy-start | bytes 98308
  439.1 252.4 %all-reduce.15.cloned.1.call-start = ((), (), s32[]{:S(2)}) async-start(), calls=%async_computation.16 | async-start | bytes 2621440 | tf_op jit(solution)/shard_map/psum | solution.py:60
  471.4 45.5 %copy-start.11 = (bf16[128,512]{1,0:T(8,128)(2,1)}, bf16[128,512]{1,0:T(8,128)(2,1)S(1)}, u32[]{:S(2)}) copy-start(bf16[128,512]{1,0:T(8,128)(2,1)S(1)} %all_gather.21) | copy-start | bytes 393220
  513.6 3.3 copy-start.16
  513.6 36.4 %copy-start.1 = (bf16[1,512,2560]{2,1,0:T(8,128)(2,1)S(1)}, bf16[1,512,2560]{2,1,0:T(8,128)(2,1)}, u32[]{:S(2)}) copy-start(bf16[1,512,2560]{2,1,0:T(8,128)(2,1)} %param.8) | copy-start | bytes 7864324
  513.7 3.3 collective-permute-start.1
  516.9 34.5 %copy-start.17 = (bf16[16,512]{1,0:T(8,128)(2,1)}, bf16[16,512]{1,0:T(8,128)(2,1)S(1)}, u32[]{:S(2)}) copy-start(bf16[16,512]{1,0:T(8,128)(2,1)S(1)} %collective-permute-done.1) | copy-start | bytes 49156
  549.4 0.7 copy-start.7
  551.4 216.3 %reduce-scatter.13.cloned.1.call-start = ((), (), s32[]{:S(2)}) async-start(), calls=%async_computation.11 | async-start | bytes 147456 | tf_op jit(solution)/shard_map/reduce_scatter | solution.py:107
  695.5 248.9 %all-reduce.11.cloned.1.call-start = ((), (), s32[]{:S(2)}) async-start(), calls=%async_computation.12 | async-start | bytes 1310720 | tf_op jit(solution)/shard_map/psum | solution.py:95
  769.0 3.1 collective-permute-start.2
  804.6 0.7 copy-start.12
  805.2 1.9 copy-start.3
  807.0 214.1 %reduce-scatter.11.cloned.1.call-start = ((), (), s32[]{:S(2)}) async-start(), calls=%async_computation.10 | async-start | bytes 147456 | tf_op jit(solution)/shard_map/reduce_scatter | solution.py:66
  808.4 136.0 %copy-start.2 = (bf16[128,2560]{1,0:T(8,128)(2,1)S(1)}, bf16[128,2560]{1,0:T(8,128)(2,1)}, u32[]{:S(2)}) copy-start(bf16[128,2560]{1,0:T(8,128)(2,1)} %all-reduce.9.cloned.1.call-done) | copy-start | bytes 1966084
  812.8 287.1 %reduce-scatter.15.cloned.1.call-start = ((), (), s32[]{:S(2)}) async-start(), calls=%async_computation.13 | async-start | bytes 147456 | tf_op jit(solution)/shard_map/reduce_scatter | solution.py:107
  948.1 331.0 %all-reduce.13.cloned.1.call-start = ((), (), s32[]{:S(2)}) async-start(), calls=%async_computation.14 | async-start | bytes 1310720 | tf_op jit(solution)/shard_map/psum | solution.py:95
  1101.3 5.5 copy-start.21
  1101.3 5.5 collective-permute-start.3
  1139.3 0.7 copy-start.9
  1141.8 213.1 %reduce-scatter.17.cloned.1.call-start = ((), (), s32[]{:S(2)}) async-start(), calls=%async_computation.15 | async-start | bytes 147456 | tf_op jit(solution)/shard_map/reduce_scatter | solution.py:107
  1142.0 4.9 copy-start.5
  1142.0 4.9 copy-start.10
  1146.9 132.3 %copy-start.6 = (bf16[128,2560]{1,0:T(8,128)(2,1)S(1)}, bf16[128,2560]{1,0:T(8,128)(2,1)}, u32[]{:S(2)}) copy-start(bf16[128,2560]{1,0:T(8,128)(2,1)} %all-reduce.7.cloned.1.call-done) | copy-start | bytes 1966084
  1282.9 2.5 copy-start.4
  1282.9 2.5 copy-start.8
  1282.9 2.5 copy-start.13
  1285.4 70.2 %copy-start.18 = (bf16[1,16,512]{2,1,0:T(8,128)(2,1)S(1)}, bf16[1,16,512]{2,1,0:T(8,128)(2,1)}, u32[]{:S(2)}) copy-start(bf16[1,16,512]{2,1,0:T(8,128)(2,1)} %get-tuple-element.6) | copy-start | bytes 49156
  1285.4 70.2 %copy-start.19 = (bf16[1,16,512]{2,1,0:T(8,128)(2,1)S(1)}, bf16[1,16,512]{2,1,0:T(8,128)(2,1)}, u32[]{:S(2)}) copy-start(bf16[1,16,512]{2,1,0:T(8,128)(2,1)} %get-tuple-element.8) | copy-start | bytes 49156
Sparse Core Ops, SparseCore 0:
  45.1 139.1 all-reduce.6
  189.2 71.8 reduce-scatter.6
  299.6 137.1 all-reduce.8
  441.0 71.8 reduce-scatter.8
  551.5 139.9 all-reduce.14
  695.8 71.8 reduce-scatter.12
  807.2 137.1 all-reduce.10
  949.3 71.7 reduce-scatter.10
  1026.1 73.8 reduce-scatter.14
  1141.9 137.1 all-reduce.12
  1283.0 71.8 reduce-scatter.16
where the time goes:
time: 1360 us
  waiting for transfers between devices  1080 us (79%)
  blocking collectives  195 us (14%)
  matrix products  58.9 us (4%)
  between operations  14.1 us (1%)
    psum x3, waiting for transfers between devices, per_device(): lax.psum(partial_value.astype(jnp.bfloat16), 'tensor').astype(jnp.float32)  416 us
    psum x2, waiting for transfers between devices, per_device(): lax.psum(back_term.astype(jnp.bfloat16), 'tensor').astype(jnp.float32)  257 us
    reduce_scatter x3, waiting for transfers between devices, per_device(): lax.psum_scatter(in_term(jnp.int32(0), local_rows * lax.axis_size('dp'))....  212 us
    reduce_scatter x3, waiting for transfers between devices, per_device(): lax.psum_scatter(out_term(jnp.int32(0), local_rows * lax.axis_size('dp'))...  189 us
    all_gather x3, blocking collectives, per_device(): gathered = lax.all_gather(tok_rows, 'dp', axis=0, tiled=True)  98.6 us
    all_gather x3, blocking collectives, per_device(): grads_full = lax.all_gather(grad_rows, 'dp', axis=0, tiled=True)  96.9 us
  transfers between devices with their start and end apart: 15, of which 13 were waited for; matrix products, arithmetic and copies ran while one was open for 3% of the time, Pallas kernels for 0%

commit v1 on v0

v1 whole, which is shorter than its diff:
```python
import functools
import math

import jax
import jax.numpy as jnp
from jax import lax
from jax.experimental import pallas as pl
from jax.experimental.pallas import tpu as pltpu
from jax.sharding import PartitionSpec as P

gelu_coef = math.sqrt(2.0 / math.pi)
MESH = pl.DeviceIdType.MESH
BF = jnp.bfloat16
F32 = jnp.float32
ROWS = 16
NY = 2

HID, BACK = 0, 1
ACT, DEL = 0, 1
OUT, THR = 0, 1
XS, IS = 0, 1


def gelu_parts(values):
    tangent = jnp.tanh(gelu_coef * (values + 0.044715 * values * values * values))
    half = 0.5 * (1.0 + tangent)
    return values * half, half + 0.5 * values * (1.0 - tangent * tangent) * gelu_coef * (
        1.0 + 3.0 * 0.044715 * values * values
    )


def power_of_two(exponent):
    return jnp.where(
        exponent == -9,
        2.0**-9,
        jnp.where(exponent == -8, 2.0**-8, jnp.where(exponent == -7, 2.0**-7, 2.0**-6)),
    ).astype(F32)


def inverse_power(exponent):
    return jnp.where(
        exponent == -9,
        2.0**9,
        jnp.where(exponent == -8, 2.0**8, jnp.where(exponent == -7, 2.0**7, 2.0**6)),
    ).astype(F32)


def column_step(width):
    return 256 if width % 256 == 0 else 128


def kernel(
    ndp,
    nz,
    x_ref,
    c_ref,
    e_ref,
    wu_hbm,
    wd_hbm,
    so_ref,
    ig_ref,
    xf_hbm,
    if_hbm,
    af_hbm,
    df_hbm,
    wu,
    wd,
    full,
    part,
    ypart,
    zsum,
    zpart,
    shard,
    wide,
    acc,
    opart,
    odp,
    handed,
    w_sem,
    g_send,
    g_recv,
    y_send,
    y_recv,
    z_send,
    z_recv,
    az_send,
    az_recv,
    ay_send,
    ay_recv,
    o_send,
    o_recv,
    h_send,
    out_sem,
):
    sec = lax.axis_index("section")
    p = lax.axis_index("dp")
    q = lax.axis_index("tensor")
    y = q // nz
    z = q % nz
    micro = x_ref.shape[0]
    tokens = ROWS * ndp
    half = wu.shape[2]
    feats = wu.shape[1]
    my_dp = pl.ds(pl.multiple_of(p * ROWS, ROWS), ROWS)
    my_z = pl.ds(pl.multiple_of(z * ROWS, ROWS), ROWS)
    partner = {"tensor": (1 - y) * nz + z}

    def rows(index):
        return pl.ds(pl.multiple_of(index * ROWS, ROWS), ROWS)

    def dp_peer(j):
        return lax.rem(p + j, ndp)

    def z_peer(d):
        return y * nz + lax.rem(z + d, nz)

    def remote(src, dst, send, recv, where):
        pltpu.make_async_remote_copy(
            src_ref=src, dst_ref=dst, send_sem=send, recv_sem=recv, device_id=where, device_id_type=MESH
        ).start()

    def await_bytes(ref, sem):
        pltpu.make_async_copy(ref, ref, sem).wait()

    loads = []
    for h in range(NY):
        loads.append(pltpu.make_async_copy(wu_hbm.at[:, pl.ds(h * half, half)], wu.at[h], w_sem.at[0, h]))
        loads.append(pltpu.make_async_copy(wd_hbm.at[pl.ds(h * half, half)], wd.at[h], w_sem.at[1, h]))
    for load in loads:
        load.start()

    barrier = pltpu.get_barrier_semaphore()

    @pl.loop(1, ndp)
    def _(j):
        pl.semaphore_signal(barrier, inc=1, device_id={"dp": dp_peer(j)}, device_id_type=MESH)

    @pl.loop(0, ndp)
    def _(j):
        pl.semaphore_signal(
            barrier, inc=1, device_id={"section": 1 - sec, "dp": dp_peer(j)}, device_id_type=MESH
        )

    @pl.loop(1, nz)
    def _(d):
        pl.semaphore_signal(barrier, inc=1, device_id={"tensor": z_peer(d)}, device_id_type=MESH)

    pl.semaphore_signal(barrier, inc=1, device_id=partner, device_id_type=MESH)
    pl.semaphore_wait(barrier, 2 * ndp + nz - 1)

    def gather_own(op, m, source):
        @pl.loop(1, ndp)
        def _(j):
            remote(
                source.at[m], full.at[op, m, my_dp], g_send.at[op, m], g_recv.at[op, m], {"dp": dp_peer(j)}
            )

        full[op, m, my_dp, :] = source[m]

    def hand_over(op, m):
        @pl.loop(0, ndp)
        def _(j):
            remote(
                handed.at[op, m],
                full.at[op, m, my_dp],
                h_send.at[op, m],
                g_recv.at[op, m],
                {"section": 1 - sec, "dp": dp_peer(j)},
            )

    def keep_full(op, m):
        dst = (xf_hbm, if_hbm)[op]
        pltpu.make_async_copy(
            full.at[op, m], dst.at[pl.ds(m * tokens, tokens)], out_sem.at[op, m]
        ).start()

    def product(op, m, h, slot):
        step = column_step(half)

        @pl.loop(0, half // step)
        def _(j):
            at = pl.ds(pl.multiple_of(j * step, step), step)
            if op == HID:
                value = jnp.dot(full[XS, m], wu[h, :, at], preferred_element_type=F32)
            else:
                value = lax.dot_general(
                    full[IS, m], wd[h, at, :], (((1,), (1,)), ((), ())), preferred_element_type=F32
                )
            part[op, m, slot, :, at] = value.astype(BF)

    def stage_a(op, m, arrivals):
        source = (XS, IS)[op]
        await_bytes(full.at[source, m, pl.ds(0, arrivals * ROWS)], g_recv.at[source, m])
        product(op, m, 1 - y, 0)

        @pl.loop(0, nz)
        def _(k):
            there = rows(lax.rem(z + ring_order(k), nz))
            remote(
                part.at[op, m, 0, there],
                ypart.at[op, m, there],
                y_send.at[op, m],
                y_recv.at[op, m, k],
                partner,
            )

        product(op, m, y, 1)
        keep_full(source, m)

    def ring_order(k):
        return nz // 2 + (1 - 2 * (k % 2)) * ((k + 1) // 2)

    def stage_b(op, m):
        def summed(k):
            there = rows(lax.rem(z + ring_order(k), nz))
            await_bytes(ypart.at[op, m, there], y_recv.at[op, m, k])
            return there, (
                part[op, m, 1, there, :].astype(F32) + ypart[op, m, there, :].astype(F32)
            ).astype(BF)

        @pl.loop(0, nz - 1)
        def _(k):
            there, value = summed(k)
            zsum[op, m, there, :] = value
            remote(
                zsum.at[op, m, there],
                zpart.at[op, m, my_z],
                z_send.at[op, m],
                z_recv.at[op, m],
                {"tensor": z_peer(ring_order(k))},
            )

        _, own = summed(nz - 1)
        zpart[op, m, my_z, :] = own

    def reduced(op, m):
        await_bytes(zpart.at[op, m, pl.ds(0, ROWS * (nz - 1))], z_recv.at[op, m])
        total = zpart[op, m, pl.ds(0, ROWS), :].astype(F32)
        for k in range(1, nz):
            total = total + zpart[op, m, pl.ds(ROWS * k, ROWS), :].astype(F32)
        return total

    def spread(op, m, value):
        wide[op, m, y, my_z, :] = value
        mine = wide.at[op, m, y, my_z]

        @pl.loop(0, nz - 1)
        def _(k):
            remote(
                mine,
                mine,
                az_send.at[op, m],
                az_recv.at[op, m, z],
                {"tensor": z_peer(ring_order(k))},
            )

        remote(mine, mine, ay_send.at[op, m], ay_recv.at[op, m], partner)

    def stage_d(op, m):
        @pl.loop(0, nz - 1)
        def _(k):
            there = lax.rem(z + ring_order(nz - 2 - k), nz)
            piece = wide.at[op, m, y, rows(there)]
            await_bytes(piece, az_recv.at[op, m, there])
            remote(piece, piece, ay_send.at[op, m], ay_recv.at[op, m], partner)

    def keep_wide(op, m):
        dst = (af_hbm, df_hbm)[op]
        for h in range(NY):
            pltpu.make_async_copy(
                wide.at[op, m, h],
                dst.at[pl.ds(m * tokens, tokens), pl.ds(h * half, half)],
                out_sem.at[2 + op, m],
            ).start()

    def stage_e(op, m):
        def dots(h, finish):
            for j in range(feats // column_step(feats)):
                at = pl.ds(j * column_step(feats), column_step(feats))
                if op == OUT:
                    value = jnp.dot(wide[op, m, h], wd[h, :, at], preferred_element_type=F32)
                else:
                    value = lax.dot_general(
                        wide[op, m, h], wu[h, at, :], (((1,), (1,)), ((), ())), preferred_element_type=F32
                    )
                finish(at, value)

        def first(at, value):
            acc[:, at] = value

        def second(at, value):
            opart[op, m, :, at] = (acc[:, at] + value).astype(BF)

        dots(y, first)
        await_bytes(wide.at[op, m, 1 - y], ay_recv.at[op, m])
        dots(1 - y, second)

        @pl.loop(1, ndp)
        def _(j):
            to = dp_peer(j)
            remote(
                opart.at[op, m, rows(to)],
                odp.at[op, m, my_dp],
                o_send.at[op, m],
                o_recv.at[op, m],
                {"dp": to},
            )

        odp[op, m, my_dp, :] = opart[op, m, my_dp, :]
        keep_wide(op, m)

    def scattered(op, m):
        await_bytes(odp.at[op, m, pl.ds(0, ROWS * (ndp - 1))], o_recv.at[op, m])
        total = odp[op, m, pl.ds(0, ROWS), :].astype(F32)
        for k in range(1, ndp):
            total = total + odp[op, m, pl.ds(ROWS * k, ROWS), :].astype(F32)
        return total

    def finish_out(m):
        value = (full[XS, m, my_dp, :].astype(F32) + scattered(OUT, m)).astype(BF)
        so_ref[m] = value
        return value

    def finish_through(m):
        through = full[IS, m, my_dp, :].astype(F32) + scattered(THR, m)
        ig_ref[m] = through.astype(BF)
        return through

    def restore(m, through):
        for i in range(e_ref.shape[1]):
            for j in range(e_ref.shape[2]):
                tile = through[8 * i : 8 * i + 8, 128 * j : 128 * j + 128]
                exponent = e_ref[m, i, j]
                packed = jnp.clip(tile * inverse_power(exponent), -448.0, 448.0).astype(BF)
                acc[pl.ds(8 * i, 8), pl.ds(128 * j, 128)] = packed.astype(F32) * power_of_two(exponent)
        handed[IS, m] = acc[pl.ds(0, ROWS), :].astype(BF)

    @pl.when(sec == 0)
    def _():
        for m in range(micro):
            gather_own(XS, m, x_ref)
        for load in loads:
            load.wait()

        def forward_c(m):
            hidden = reduced(HID, m)
            shard[HID, m] = hidden
            spread(ACT, m, gelu_parts(hidden)[0].astype(BF))

        def forward_f(m):
            handed[XS, m] = finish_out(m)
            hand_over(XS, m)

        def backward_c(m):
            delta = reduced(BACK, m) * gelu_parts(shard[HID, m])[1]
            spread(DEL, m, delta.astype(BF))

        stage_a(HID, 0, ndp - 1)
        stage_a(HID, 1, ndp - 1)
        stage_b(HID, 0)
        stage_b(HID, 1)
        forward_c(0)
        forward_c(1)
        stage_d(ACT, 0)
        stage_e(OUT, 0)
        stage_d(ACT, 1)
        forward_f(0)
        stage_e(OUT, 1)
        forward_f(1)

        stage_a(BACK, 0, ndp)
        stage_b(BACK, 0)
        backward_c(0)
        stage_a(BACK, 1, ndp)
        stage_d(DEL, 0)
        stage_b(BACK, 1)
        stage_e(THR, 0)
        backward_c(1)
        finish_through(0)
        stage_d(DEL, 1)
        stage_e(THR, 1)
        finish_through(1)

    @pl.when(sec == 1)
    def _():
        for m in range(micro):
            gather_own(IS, m, c_ref)
        for load in loads:
            load.wait()

        def early_c(m):
            shard[BACK, m] = reduced(BACK, m)

        def turn_c(m):
            active, slope = gelu_parts(reduced(HID, m))
            spread(DEL, m, (shard[BACK, m] * slope).astype(BF))
            shard[HID, m] = active

        def turn_f(m):
            restore(m, finish_through(m))
            hand_over(IS, m)

        stage_a(BACK, 0, ndp - 1)
        stage_a(BACK, 1, ndp - 1)
        stage_b(BACK, 0)
        stage_b(BACK, 1)
        early_c(0)
        early_c(1)

        stage_a(HID, 0, ndp)
        stage_b(HID, 0)
        turn_c(0)
        stage_a(HID, 1, ndp)
        stage_d(DEL, 0)
        stage_b(HID, 1)
        stage_e(THR, 0)
        turn_c(1)
        turn_f(0)
        stage_d(DEL, 1)
        stage_e(THR, 1)
        turn_f(1)

        for m in range(micro):
            spread(ACT, m, shard[HID, m].astype(BF))
        for m in range(micro):
            stage_d(ACT, m)
        for m in range(micro):
            stage_e(OUT, m)
        for m in range(micro):
            finish_out(m)

    for m in range(micro):
        for op in range(2):
            await_bytes(part.at[op, m, 0], y_send.at[op, m])
            await_bytes(zsum.at[op, m, pl.ds(0, ROWS * (nz - 1))], z_send.at[op, m])
            await_bytes(wide.at[op, m, 0, pl.ds(0, ROWS * (nz - 1))], az_send.at[op, m])
            await_bytes(wide.at[op, m, 0], ay_send.at[op, m])
            await_bytes(opart.at[op, m, pl.ds(0, ROWS * (ndp - 1))], o_send.at[op, m])
            await_bytes(full.at[op, m], out_sem.at[op, m])
            await_bytes(wide.at[op, m], out_sem.at[2 + op, m])

        @pl.when(sec == 0)
        def _():
            await_bytes(full.at[XS, m, pl.ds(0, ROWS * (ndp - 1))], g_send.at[XS, m])
            await_bytes(full.at[XS, m], h_send.at[XS, m])

        @pl.when(sec == 1)
        def _():
            await_bytes(full.at[IS, m, pl.ds(0, ROWS * (ndp - 1))], g_send.at[IS, m])
            await_bytes(full.at[IS, m], h_send.at[IS, m])


def per_device(ndp, ntensor, inputs, cotangent, scale_exps, up_weight, down_weight):
    nz = ntensor // NY
    micro, own_rows, feats = inputs.shape
    units = up_weight.shape[2]
    half = units // NY
    tokens = own_rows * ndp
    vmem = pl.BlockSpec(memory_space=pltpu.VMEM)
    anywhere = pl.BlockSpec(memory_space=pl.ANY)
    dma = pltpu.SemaphoreType.DMA
    section_out, input_grads, x_full, i_full, active, delta = pl.pallas_call(
        functools.partial(kernel, ndp, nz),
        out_shape=[
            jax.ShapeDtypeStruct(inputs.shape, BF),
            jax.ShapeDtypeStruct(inputs.shape, BF),
            jax.ShapeDtypeStruct((micro * tokens, feats), BF),
            jax.ShapeDtypeStruct((micro * tokens, feats), BF),
            jax.ShapeDtypeStruct((micro * tokens, units), BF),
            jax.ShapeDtypeStruct((micro * tokens, units), BF),
        ],
        in_specs=[vmem, vmem, pl.BlockSpec(memory_space=pltpu.SMEM), anywhere, anywhere],
        out_specs=[vmem, vmem, anywhere, anywhere, anywhere, anywhere],
        scratch_shapes=[
            pltpu.VMEM((NY, feats, half), BF),
            pltpu.VMEM((NY, half, feats), BF),
            pltpu.VMEM((2, micro, tokens, feats), BF),
            pltpu.VMEM((2, micro, 2, tokens, half), BF),
            pltpu.VMEM((2, micro, tokens, half), BF),
            pltpu.VMEM((2, micro, tokens, half), BF),
            pltpu.VMEM((2, micro, nz * ROWS, half), BF),
            pltpu.VMEM((2, micro, ROWS, half), F32),
            pltpu.VMEM((2, micro, NY, tokens, half), BF),
            pltpu.VMEM((tokens, feats), F32),
            pltpu.VMEM((2, micro, tokens, feats), BF),
            pltpu.VMEM((2, micro, tokens, feats), BF),
            pltpu.VMEM((2, micro, ROWS, feats), BF),
            dma((2, NY)),
            dma((2, micro)),
            dma((2, micro)),
            dma((2, micro)),
            dma((2, micro, nz)),
            dma((2, micro)),
            dma((2, micro)),
            dma((2, micro)),
            dma((2, micro, nz)),
            dma((2, micro)),
            dma((2, micro)),
            dma((2, micro)),
            dma((2, micro)),
            dma((2, micro)),
            dma((4, micro)),
        ],
        compiler_params=pltpu.CompilerParams(
            collective_id=0, has_side_effects=True, vmem_limit_bytes=48 * 1024 * 1024
        ),
        name="relay",
    )(inputs, cotangent, scale_exps, up_weight[0], down_weight[0])
    over_tokens = (((0,), (0,)), ((), ()))
    up_grads = lax.dot_general(x_full, delta, over_tokens, preferred_element_type=F32).astype(BF)
    down_grads = lax.dot_general(active, i_full, over_tokens, preferred_element_type=F32).astype(BF)
    return section_out[None], input_grads[None], up_grads[None], down_grads[None]


def solution(mesh):
    in_specs = (
        P(None, "dp", "tensor"),
        P(None, "dp", "tensor"),
        P(None, "dp", "tensor"),
        P("section", "tensor", "dp"),
        P("section", "dp", "tensor"),
    )
    out_specs = (
        P("section", None, "dp", "tensor"),
        P("section", None, "dp", "tensor"),
        P("section", "tensor", "dp"),
        P("section", "dp", "tensor"),
    )
    return jax.shard_map(
        functools.partial(per_device, mesh.shape["dp"], mesh.shape["tensor"]),
        mesh=mesh,
        in_specs=in_specs,
        out_specs=out_specs,
        check_vma=False,
    )
```

time: 1360 us -> 146 us (0.11)
  waiting for transfers between devices: 1080 us -> 0 us
  blocking collectives: 195 us -> 0 us
  Pallas kernels: 0 us -> 135 us
  matrix products: 58.9 us -> 4.73 us
    psum x5 -> x0, waiting for transfers between devices: 673 us -> none  [the longest x3 416 us: per_device(): lax.psum(partial_value.astype(jnp.bfloat16), 'tensor').astype(jnp.float32)]
    reduce_scatter x6 -> x0, waiting for transfers between devices: 401 us -> none  [the longest x3 212 us: per_device(): lax.psum_scatter(in_term(jnp.int32(0), local_rows * lax.axis_size('dp'))....]
    all_gather x6 -> x0, blocking collectives: 195 us -> none  [the longest x3 98.6 us: per_device(): gathered = lax.all_gather(tok_rows, 'dp', axis=0, tiled=True)]
    pallas_call x0 -> x1, Pallas kernels: none -> 135 us  [per_device(): pl.pallas_call(functools.partial(kernel, ndp, nz), out_shape=[jax.ShapeDt...]
    dot_general x18 -> x2, matrix products: 58.9 us -> 4.73 us  [the longest x1 2.36 us: per_device(): lax.dot_general(x_full, delta, over_tokens, preferred_element_type=F32)]
  transfers between devices with their start and end apart: 15 -> 0, of which waited for: 13 -> 0; matrix products, arithmetic and copies ran while one was open for 3% -> 0% of each run, Pallas kernels for 0% -> 0%
where the time goes in v1:
time: 146 us; the launch traced here: 145 us
  Pallas kernels  135 us (92%)
  local copies, waits for them, and re-layouts  5.16 us (4%)
  matrix products  4.73 us (3%)
    pallas_call x1, Pallas kernels, per_device(): pl.pallas_call(functools.partial(kernel, ndp, nz), out_shape=[jax.ShapeDt...  135 us
    unnamed x10, local copies, waits for them, and re-layouts  5.16 us

profile of v1, /device:TPU:2, one launch (start us, length us, event | category | flops | bytes accessed | tf_op | source)
XLA Modules:
  0.0 145.2 jit_solution(13184396609616837975)
XLA Ops:
  0.6 0.0 copy-start
  0.6 1.7 %copy-done = bf16[1,512,2560]{2,1,0:T(8,128)(2,1)S(1)} copy-done((bf16[1,512,2560]{2,1,0:T(8,128)(2,1)S(1)}, bf16[1,512,2560]{2,1,0:T(8,128)(2,1)}, u32[]{:S(2)}) %copy-start) | copy-done | bytes 2621464
  2.4 0.0 copy-start.1
  2.4 0.8 copy-done.1
  3.1 0.0 copy-start.2
  3.1 0.8 copy-done.2
  3.9 0.0 copy-start.3
  3.9 0.7 copy-done.3
  4.6 134.7 %relay.1 = (bf16[2,16,512]{2,1,0:T(8,128)(2,1)S(1)}, bf16[2,16,512]{2,1,0:T(8,128)(2,1)S(1)}, bf16[256,512]{1,0:T(8,128)(2,1)S(1)}, bf16[256,512]{1,0:T(8,128)(2...) custom-call(bf16[2,16,512]{2,1,0:T(8,128)(2,1)S(1)} %copy-done.1, ...), custom_call_target="tpu_custom_call" | custom-call | tf_op jit(solution)/shard_map/relay/pallas_call | solution.py:462
  139.3 2.4 %fusion = bf16[1,512,2560]{2,1,0:T(8,128)(2,1)} fusion(bf16[256,512]{1,0:T(8,128)(2,1)S(1)} %get-tuple-element.12, bf16[256,2560]{1,0:T(8,128)(2,1)S(1)} %get-tuple-element.13), kind=kOutput, calls=%fused_computation.2 | convolution fusion | flops 672399360 | bytes 4194304 | tf_op jit(solution)/shard_map/dot_general | solution.py:510
  141.6 2.4 %fusion.1 = bf16[1,2560,512]{2,1,0:T(8,128)(2,1)} fusion(bf16[256,2560]{1,0:T(8,128)(2,1)S(1)} %get-tuple-element.14, bf16[256,512]{1,0:T(8,128)(2,1)S(1)} %get-tuple-element.15), kind=kOutput, calls=%fused_computation.3 | convolution fusion | flops 672399360 | bytes 4194304 | tf_op jit(solution)/shard_map/dot_general | solution.py:511
  144.0 0.6 copy.11
  144.6 0.6 copy.12
Async XLA Ops:
  0.6 1.7 %copy-start = (bf16[1,512,2560]{2,1,0:T(8,128)(2,1)S(1)}, bf16[1,512,2560]{2,1,0:T(8,128)(2,1)}, u32[]{:S(2)}) copy-start(bf16[1,512,2560]{2,1,0:T(8,128)(2,1)} %param.8) | copy-start | bytes 7864324
  2.4 0.8 copy-start.1
  3.1 0.8 copy-start.2
  3.9 0.7 copy-start.3

commit v2 on v1

--- a/solution.py
+++ b/solution.py
@@ -21,6 +21,11 @@
 XS, IS = 0, 1
 
 
+START = 0
+LOCK = ("a0", "a1", "b0", "b1", "c0", "c1", "d0", "d1", "e0", "e1", "f0", "f1")
+ORDER0, ORDER1, ORDER2, ORDERB = LOCK, LOCK, LOCK, LOCK[:6]
+
+
 def gelu_parts(values):
     tangent = jnp.tanh(gelu_coef * (values + 0.044715 * values * values * values))
     half = 0.5 * (1.0 + tangent)
@@ -52,17 +57,15 @@
 def kernel(
     ndp,
     nz,
-    x_ref,
-    c_ref,
-    e_ref,
+    x_hbm,
+    c_hbm,
+    e_hbm,
     wu_hbm,
     wd_hbm,
     so_ref,
     ig_ref,
-    xf_hbm,
-    if_hbm,
-    af_hbm,
-    df_hbm,
+    ug_ref,
+    dg_ref,
     wu,
     wd,
     full,
@@ -76,7 +79,11 @@
     opart,
     odp,
     handed,
+    turned,
+    e_ref,
     w_sem,
+    r_sem,
+    e_sem,
     g_send,
     g_recv,
     y_send,
@@ -90,14 +97,14 @@
     o_send,
     o_recv,
     h_send,
-    out_sem,
+    start_sem,
 ):
     sec = lax.axis_index("section")
     p = lax.axis_index("dp")
     q = lax.axis_index("tensor")
     y = q // nz
     z = q % nz
-    micro = x_ref.shape[0]
+    micro = x_hbm.shape[0]
     tokens = ROWS * ndp
     half = wu.shape[2]
     feats = wu.shape[1]
@@ -108,8 +115,15 @@
     def rows(index):
         return pl.ds(pl.multiple_of(index * ROWS, ROWS), ROWS)
 
+    nx = ndp // NY
+
+    def ring_order(k, n):
+        return n // 2 + (1 - 2 * (k % 2)) * ((k + 1) // 2)
+
     def dp_peer(j):
-        return lax.rem(p + j, ndp)
+        across_y = 1 - j // nx
+        x = lax.rem(p // NY + ring_order(lax.rem(j, nx), nx), nx)
+        return x * NY + lax.rem(p + across_y, NY)
 
     def z_peer(d):
         return y * nz + lax.rem(z + d, nz)
@@ -128,10 +142,25 @@
         loads.append(pltpu.make_async_copy(wd_hbm.at[pl.ds(h * half, half)], wd.at[h], w_sem.at[1, h]))
     for load in loads:
         load.start()
+    scales = pltpu.make_async_copy(e_hbm, e_ref, e_sem)
+    scales.start()
+
+    def own_rows(op):
+        source = (x_hbm, c_hbm)[op]
+        return [
+            pltpu.make_async_copy(source.at[m], full.at[op, m, my_dp], r_sem.at[m]) for m in range(micro)
+        ]
+
+    for op in (XS, IS):
+
+        @pl.when(sec == op)
+        def _():
+            for load in own_rows(op):
+                load.start()
 
     barrier = pltpu.get_barrier_semaphore()
 
-    @pl.loop(1, ndp)
+    @pl.loop(0, ndp - 1)
     def _(j):
         pl.semaphore_signal(barrier, inc=1, device_id={"dp": dp_peer(j)}, device_id_type=MESH)
 
@@ -148,14 +177,14 @@
     pl.semaphore_signal(barrier, inc=1, device_id=partner, device_id_type=MESH)
     pl.semaphore_wait(barrier, 2 * ndp + nz - 1)
 
-    def gather_own(op, m, source):
-        @pl.loop(1, ndp)
-        def _(j):
-            remote(
-                source.at[m], full.at[op, m, my_dp], g_send.at[op, m], g_recv.at[op, m], {"dp": dp_peer(j)}
-            )
-
-        full[op, m, my_dp, :] = source[m]
+    def gather_own(op):
+        for m, load in enumerate(own_rows(op)):
+            load.wait()
+            mine = full.at[op, m, my_dp]
+
+            @pl.loop(0, ndp - 1)
+            def _(j):
+                remote(mine, mine, g_send.at[op, m], g_recv.at[op, m], {"dp": dp_peer(j)})
 
     def hand_over(op, m):
         @pl.loop(0, ndp)
@@ -168,18 +197,10 @@
                 {"section": 1 - sec, "dp": dp_peer(j)},
             )
 
-    def keep_full(op, m):
-        dst = (xf_hbm, if_hbm)[op]
-        pltpu.make_async_copy(
-            full.at[op, m], dst.at[pl.ds(m * tokens, tokens)], out_sem.at[op, m]
-        ).start()
-
     def product(op, m, h, slot):
         step = column_step(half)
-
-        @pl.loop(0, half // step)
-        def _(j):
-            at = pl.ds(pl.multiple_of(j * step, step), step)
+        for j in range(half // step):
+            at = pl.ds(j * step, step)
             if op == HID:
                 value = jnp.dot(full[XS, m], wu[h, :, at], preferred_element_type=F32)
             else:
@@ -188,14 +209,16 @@
                 )
             part[op, m, slot, :, at] = value.astype(BF)
 
-    def stage_a(op, m, arrivals):
+    def stage_a(op, m, arrivals, before_sends=None):
         source = (XS, IS)[op]
         await_bytes(full.at[source, m, pl.ds(0, arrivals * ROWS)], g_recv.at[source, m])
         product(op, m, 1 - y, 0)
+        if before_sends is not None:
+            before_sends()
 
         @pl.loop(0, nz)
         def _(k):
-            there = rows(lax.rem(z + ring_order(k), nz))
+            there = rows(lax.rem(z + ring_order(k, nz), nz))
             remote(
                 part.at[op, m, 0, there],
                 ypart.at[op, m, there],
@@ -205,39 +228,36 @@
             )
 
         product(op, m, y, 1)
-        keep_full(source, m)
-
-    def ring_order(k):
-        return nz // 2 + (1 - 2 * (k % 2)) * ((k + 1) // 2)
-
-    def stage_b(op, m):
+
+    def stage_b(op, m, low, high):
         def summed(k):
-            there = rows(lax.rem(z + ring_order(k), nz))
+            there = rows(lax.rem(z + ring_order(k, nz), nz))
             await_bytes(ypart.at[op, m, there], y_recv.at[op, m, k])
             return there, (
                 part[op, m, 1, there, :].astype(F32) + ypart[op, m, there, :].astype(F32)
             ).astype(BF)
 
-        @pl.loop(0, nz - 1)
+        @pl.loop(low, min(high, nz - 1))
         def _(k):
             there, value = summed(k)
             zsum[op, m, there, :] = value
             remote(
                 zsum.at[op, m, there],
-                zpart.at[op, m, my_z],
+                zpart.at[op, m, k],
                 z_send.at[op, m],
                 z_recv.at[op, m],
-                {"tensor": z_peer(ring_order(k))},
+                {"tensor": z_peer(ring_order(k, nz))},
             )
 
-        _, own = summed(nz - 1)
-        zpart[op, m, my_z, :] = own
+        if high == nz:
+            _, own = summed(nz - 1)
+            zpart[op, m, nz - 1] = own
 
     def reduced(op, m):
-        await_bytes(zpart.at[op, m, pl.ds(0, ROWS * (nz - 1))], z_recv.at[op, m])
-        total = zpart[op, m, pl.ds(0, ROWS), :].astype(F32)
-        for k in range(1, nz):
-            total = total + zpart[op, m, pl.ds(ROWS * k, ROWS), :].astype(F32)
+        await_bytes(zpart.at[op, m, pl.ds(0, nz - 1)], z_recv.at[op, m])
+        total = zpart[op, m, nz - 1].astype(F32)
+        for k in range(nz - 1):
+            total = total + zpart[op, m, k].astype(F32)
         return total
 
     def spread(op, m, value):
@@ -251,27 +271,18 @@
                 mine,
                 az_send.at[op, m],
                 az_recv.at[op, m, z],
-                {"tensor": z_peer(ring_order(k))},
+                {"tensor": z_peer(ring_order(k, nz))},
             )
 
         remote(mine, mine, ay_send.at[op, m], ay_recv.at[op, m], partner)
 
-    def stage_d(op, m):
-        @pl.loop(0, nz - 1)
+    def stage_d(op, m, low, high):
+        @pl.loop(low, min(high, nz - 1))
         def _(k):
-            there = lax.rem(z + ring_order(nz - 2 - k), nz)
+            there = lax.rem(z + ring_order(nz - 2 - k, nz), nz)
             piece = wide.at[op, m, y, rows(there)]
             await_bytes(piece, az_recv.at[op, m, there])
             remote(piece, piece, ay_send.at[op, m], ay_recv.at[op, m], partner)
-
-    def keep_wide(op, m):
-        dst = (af_hbm, df_hbm)[op]
-        for h in range(NY):
-            pltpu.make_async_copy(
-                wide.at[op, m, h],
-                dst.at[pl.ds(m * tokens, tokens), pl.ds(h * half, half)],
-                out_sem.at[2 + op, m],
-            ).start()
 
     def stage_e(op, m):
         def dots(h, finish):
@@ -295,7 +306,7 @@
         await_bytes(wide.at[op, m, 1 - y], ay_recv.at[op, m])
         dots(1 - y, second)
 
-        @pl.loop(1, ndp)
+        @pl.loop(0, ndp - 1)
         def _(j):
             to = dp_peer(j)
             remote(
@@ -307,7 +318,6 @@
             )
 
         odp[op, m, my_dp, :] = opart[op, m, my_dp, :]
-        keep_wide(op, m)
 
     def scattered(op, m):
         await_bytes(odp.at[op, m, pl.ds(0, ROWS * (ndp - 1))], o_recv.at[op, m])
@@ -335,58 +345,94 @@
                 acc[pl.ds(8 * i, 8), pl.ds(128 * j, 128)] = packed.astype(F32) * power_of_two(exponent)
         handed[IS, m] = acc[pl.ds(0, ROWS), :].astype(BF)
 
+    def up_gradient():
+        turned[...] = full[XS].reshape(micro * tokens, feats).T
+        step = column_step(half)
+        for h in range(NY):
+            for j in range(half // step):
+                right = wide[DEL, :, h, :, pl.ds(j * step, step)].reshape(micro * tokens, step)
+                ug_ref[:, pl.ds(h * half + j * step, step)] = jnp.dot(
+                    turned[...], right, preferred_element_type=F32
+                ).astype(BF)
+
+    def down_gradient():
+        step = column_step(half)
+        for h in range(NY):
+            for j in range(half // step):
+                left = wide[ACT, :, h, :, pl.ds(j * step, step)].reshape(micro * tokens, step)
+                dg_ref[pl.ds(h * half + j * step, step), :] = lax.dot_general(
+                    left,
+                    full[IS].reshape(micro * tokens, feats),
+                    (((0,), (0,)), ((), ())),
+                    preferred_element_type=F32,
+                ).astype(BF)
+
+    def run(order, a, b, c, d=None, e=None, f=None):
+        for entry in order:
+            name, m = entry[0], int(entry[1])
+            if name in "bd":
+                low, high = entry[2:].split("-") if len(entry) > 2 else (0, nz)
+                {"b": b, "d": d}[name](m, min(int(low), nz), min(int(high), nz))
+            else:
+                {"a": a, "c": c, "e": e, "f": f}[name](m)
+
+    def stages(first, op, wide_op, opart_op):
+        return (
+            lambda m: stage_a(op, m, ndp if not first else ndp - 1),
+            lambda m, low, high: stage_b(op, m, low, high),
+            lambda m, low, high: stage_d(wide_op, m, low, high),
+            lambda m: stage_e(opart_op, m),
+        )
+
     @pl.when(sec == 0)
     def _():
-        for m in range(micro):
-            gather_own(XS, m, x_ref)
+        gather_own(XS)
         for load in loads:
             load.wait()
+        scales.wait()
 
         def forward_c(m):
-            hidden = reduced(HID, m)
-            shard[HID, m] = hidden
-            spread(ACT, m, gelu_parts(hidden)[0].astype(BF))
+            active, slope = gelu_parts(reduced(HID, m))
+            spread(ACT, m, active.astype(BF))
+            shard[HID, m] = slope
 
         def forward_f(m):
             handed[XS, m] = finish_out(m)
             hand_over(XS, m)
 
         def backward_c(m):
-            delta = reduced(BACK, m) * gelu_parts(shard[HID, m])[1]
-            spread(DEL, m, delta.astype(BF))
-
-        stage_a(HID, 0, ndp - 1)
-        stage_a(HID, 1, ndp - 1)
-        stage_b(HID, 0)
-        stage_b(HID, 1)
-        forward_c(0)
-        forward_c(1)
-        stage_d(ACT, 0)
-        stage_e(OUT, 0)
-        stage_d(ACT, 1)
-        forward_f(0)
-        stage_e(OUT, 1)
-        forward_f(1)
-
-        stage_a(BACK, 0, ndp)
-        stage_b(BACK, 0)
-        backward_c(0)
-        stage_a(BACK, 1, ndp)
-        stage_d(DEL, 0)
-        stage_b(BACK, 1)
-        stage_e(THR, 0)
-        backward_c(1)
-        finish_through(0)
-        stage_d(DEL, 1)
-        stage_e(THR, 1)
-        finish_through(1)
+            spread(DEL, m, (reduced(BACK, m) * shard[HID, m]).astype(BF))
+
+        def backward_e(m):
+            stage_e(THR, m)
+            if m == micro - 1:
+                up_gradient()
+
+        def start_other(m):
+            if m == START:
+                pl.semaphore_signal(start_sem, inc=1, device_id={"section": 1}, device_id_type=MESH)
+            stage_e(OUT, m)
+
+        a, b, d, _e = stages(True, HID, ACT, OUT)
+        run(ORDER0, a, b, forward_c, d, start_other, forward_f)
+        a, b_last, d, _e = stages(False, BACK, DEL, THR)
+
+        def b(m, low, high):
+            b_last(m, low, high)
+            if m == micro - 1 and high == nz:
+                down_gradient()
+
+        run(ORDER2, a, b, backward_c, d, backward_e, finish_through)
 
     @pl.when(sec == 1)
     def _():
-        for m in range(micro):
-            gather_own(IS, m, c_ref)
+        gather_own(IS)
         for load in loads:
             load.wait()
+        scales.wait()
+
+        def early_a(m):
+            stage_a(BACK, m, ndp - 1, wait_start if m == 0 else None)
 
         def early_c(m):
             shard[BACK, m] = reduced(BACK, m)
@@ -400,32 +446,25 @@
             restore(m, finish_through(m))
             hand_over(IS, m)
 
-        stage_a(BACK, 0, ndp - 1)
-        stage_a(BACK, 1, ndp - 1)
-        stage_b(BACK, 0)
-        stage_b(BACK, 1)
-        early_c(0)
-        early_c(1)
-
-        stage_a(HID, 0, ndp)
-        stage_b(HID, 0)
-        turn_c(0)
-        stage_a(HID, 1, ndp)
-        stage_d(DEL, 0)
-        stage_b(HID, 1)
-        stage_e(THR, 0)
-        turn_c(1)
-        turn_f(0)
-        stage_d(DEL, 1)
-        stage_e(THR, 1)
-        turn_f(1)
-
+        def wait_start():
+            pl.semaphore_wait(start_sem, 1)
+
+        def late_c(m):
+            spread(ACT, m, shard[HID, m].astype(BF))
+
+        a, b, d, e = stages(True, BACK, DEL, THR)
+        run(ORDERB, early_a, b, early_c)
+        a, b, d, e = stages(False, HID, DEL, THR)
+        run(ORDER1, a, b, turn_c, d, e, turn_f)
+
+        late_c(0)
+        late_c(1)
+        up_gradient()
         for m in range(micro):
-            spread(ACT, m, shard[HID, m].astype(BF))
-        for m in range(micro):
-            stage_d(ACT, m)
+            stage_d(ACT, m, 0, nz)
         for m in range(micro):
             stage_e(OUT, m)
+        down_gradient()
         for m in range(micro):
             finish_out(m)
 
@@ -436,8 +475,6 @@
             await_bytes(wide.at[op, m, 0, pl.ds(0, ROWS * (nz - 1))], az_send.at[op, m])
             await_bytes(wide.at[op, m, 0], ay_send.at[op, m])
             await_bytes(opart.at[op, m, pl.ds(0, ROWS * (ndp - 1))], o_send.at[op, m])
-            await_bytes(full.at[op, m], out_sem.at[op, m])
-            await_bytes(wide.at[op, m], out_sem.at[2 + op, m])
 
         @pl.when(sec == 0)
         def _():
@@ -448,6 +485,18 @@
         def _():
             await_bytes(full.at[IS, m, pl.ds(0, ROWS * (ndp - 1))], g_send.at[IS, m])
             await_bytes(full.at[IS, m], h_send.at[IS, m])
+
+
+def flush(*refs):
+    arrays = len(refs) // 2
+    sems = refs[-1]
+    copies = [
+        pltpu.make_async_copy(refs[i], refs[arrays + i], sems.at[i]) for i in range(arrays)
+    ]
+    for copy in copies:
+        copy.start()
+    for copy in copies:
+        copy.wait()
 
 
 def per_device(ndp, ntensor, inputs, cotangent, scale_exps, up_weight, down_weight):
@@ -457,20 +506,18 @@
     half = units // NY
     tokens = own_rows * ndp
     vmem = pl.BlockSpec(memory_space=pltpu.VMEM)
-    anywhere = pl.BlockSpec(memory_space=pl.ANY)
+    far = pl.BlockSpec(memory_space=pltpu.HBM)
     dma = pltpu.SemaphoreType.DMA
-    section_out, input_grads, x_full, i_full, active, delta = pl.pallas_call(
+    results = pl.pallas_call(
         functools.partial(kernel, ndp, nz),
         out_shape=[
             jax.ShapeDtypeStruct(inputs.shape, BF),
             jax.ShapeDtypeStruct(inputs.shape, BF),
-            jax.ShapeDtypeStruct((micro * tokens, feats), BF),
-            jax.ShapeDtypeStruct((micro * tokens, feats), BF),
-            jax.ShapeDtypeStruct((micro * tokens, units), BF),
-            jax.ShapeDtypeStruct((micro * tokens, units), BF),
+            jax.ShapeDtypeStruct((feats, units), BF),
+            jax.ShapeDtypeStruct((units, feats), BF),
         ],
-        in_specs=[vmem, vmem, pl.BlockSpec(memory_space=pltpu.SMEM), anywhere, anywhere],
-        out_specs=[vmem, vmem, anywhere, anywhere, anywhere, anywhere],
+        in_specs=[far] * 5,
+        out_specs=[vmem] * 4,
         scratch_shapes=[
             pltpu.VMEM((NY, feats, half), BF),
             pltpu.VMEM((NY, half, feats), BF),
@@ -478,14 +525,18 @@
             pltpu.VMEM((2, micro, 2, tokens, half), BF),
             pltpu.VMEM((2, micro, tokens, half), BF),
             pltpu.VMEM((2, micro, tokens, half), BF),
-            pltpu.VMEM((2, micro, nz * ROWS, half), BF),
+            pltpu.VMEM((2, micro, nz, ROWS, half), BF),
             pltpu.VMEM((2, micro, ROWS, half), F32),
             pltpu.VMEM((2, micro, NY, tokens, half), BF),
             pltpu.VMEM((tokens, feats), F32),
             pltpu.VMEM((2, micro, tokens, feats), BF),
             pltpu.VMEM((2, micro, tokens, feats), BF),
             pltpu.VMEM((2, micro, ROWS, feats), BF),
+            pltpu.VMEM((feats, micro * tokens), BF),
+            pltpu.SMEM(scale_exps.shape, jnp.int32),
             dma((2, NY)),
+            dma((micro,)),
+            dma,
             dma((2, micro)),
             dma((2, micro)),
             dma((2, micro)),
@@ -499,16 +550,22 @@
             dma((2, micro)),
             dma((2, micro)),
             dma((2, micro)),
-            dma((4, micro)),
+            pltpu.SemaphoreType.REGULAR,
         ],
         compiler_params=pltpu.CompilerParams(
             collective_id=0, has_side_effects=True, vmem_limit_bytes=48 * 1024 * 1024
         ),
         name="relay",
-    )(inputs, cotangent, scale_exps, up_weight[0], down_weight[0])
-    over_tokens = (((0,), (0,)), ((), ()))
-    up_grads = lax.dot_general(x_full, delta, over_tokens, preferred_element_type=F32).astype(BF)
-    down_grads = lax.dot_general(active, i_full, over_tokens, preferred_element_type=F32).astype(BF)
+    )(*[pltpu.with_memory_space_constraint(a, pltpu.HBM) for a in (inputs, cotangent, scale_exps, up_weight[0], down_weight[0])])
+    section_out, input_grads, up_grads, down_grads = pl.pallas_call(
+        flush,
+        out_shape=[jax.ShapeDtypeStruct(result.shape, result.dtype) for result in results],
+        in_specs=[vmem] * 4,
+        out_specs=[pl.BlockSpec(memory_space=pl.ANY)] * 4,
+        scratch_shapes=[dma((4,))],
+        compiler_params=pltpu.CompilerParams(vmem_limit_bytes=1024 * 1024),
+        name="flush",
+    )(*[pltpu.with_memory_space_constraint(result, pltpu.VMEM) for result in results])
     return section_out[None], input_grads[None], up_grads[None], down_grads[None]
 
 

time: 146 us -> 122 us (0.84)
  Pallas kernels: 135 us -> 121 us
  local copies, waits for them, and re-layouts: 5.16 us -> 0 us
  matrix products: 4.73 us -> 0 us
    pallas_call x1, Pallas kernels: 135 us -> 119 us  [per_device(): pl.pallas_call(functools.partial(kernel, ndp, nz), out_shape=[jax.ShapeDt...]
    unnamed x10 -> x0, local copies, waits for them, and re-layouts: 5.16 us -> none
    dot_general x2 -> x0, matrix products: 4.73 us -> none  [the longest x1 2.36 us: per_device(): lax.dot_general(x_full, delta, over_tokens, preferred_element_type=F32)]
    pallas_call x0 -> x1, Pallas kernels: none -> 2.41 us  [per_device(): pl.pallas_call(flush, out_shape=[jax.ShapeDtypeStruct(result.shape, resul...]
where the time goes in v2:
time: 122 us
  Pallas kernels  121 us (99%)
    pallas_call x1, Pallas kernels, per_device(): pl.pallas_call(functools.partial(kernel, ndp, nz), out_shape=[jax.ShapeDt...  119 us

profile of v2, /device:TPU:2, one launch (start us, length us, event | category | flops | bytes accessed | tf_op | source)
XLA Modules:
  0.0 122.2 jit_solution(13948380745735846201)
XLA Ops:
  0.6 119.0 %relay.1 = (bf16[2,16,512]{2,1,0:T(8,128)(2,1)S(1)}, bf16[2,16,512]{2,1,0:T(8,128)(2,1)S(1)}, bf16[512,2560]{1,0:T(8,128)(2,1)S(1)}, bf16[2560,512]{1,0:T(8,128)(2,1)S(1)}) custom-call(bf16[2,16,512]{2,1,0:T(8,128)(2,1)} %x_hbm.1, bf16[2,16,512]{2,1,0:T(8,128)(2,1)} %c_hbm.1, s32[2,2,4]{2,1,0:T(2,128)} %e_hbm.1, bf16[512,2560]{1,0:T(8,128)(2,1)} %bitcast.6, ...), custom_call_target="tpu_custom_call" | custom-call | tf_op jit(solution)/shard_map/relay/pallas_call | solution.py:511
  119.6 2.4 %flush.1 = (bf16[2,16,512]{2,1,0:T(8,128)(2,1)}, bf16[2,16,512]{2,1,0:T(8,128)(2,1)}, bf16[512,2560]{1,0:T(8,128)(2,1)}, bf16[2560,512]{1,0:T(8,128)(2,1)}) custom-call(bf16[2,16,512]{2,1,0:T(8,128)(2,1)S(1)} %get-tuple-element.12.refs_0_, bf16[2,16,512]{2,1,0:T(8,128)(2,1)S(1)} %get-tuple-element.13.refs_1_, ...), custom_call_target="tpu_custom_call" | custom-call | tf_op jit(solution)/shard_map/flush/pallas_call | solution.py:560

commit v3 on v2

v3 whole, which is shorter than its diff:
```python
import functools
import math

import jax
import jax.numpy as jnp
from jax import lax
from jax.experimental import pallas as pl
from jax.experimental.pallas import tpu as pltpu
from jax.sharding import PartitionSpec as P

gelu_coef = math.sqrt(2.0 / math.pi)
MESH = pl.DeviceIdType.MESH
BF = jnp.bfloat16
F32 = jnp.float32
ROWS = 16
NY = 2

HID, BACK = 0, 1
ACT, DEL = 0, 1
OUT, THR = 0, 1
XS, IS = 0, 1


RELAY_AT = 3
CUTS = 2


def gelu_parts(values):
    tangent = jnp.tanh(gelu_coef * (values + 0.044715 * values * values * values))
    half = 0.5 * (1.0 + tangent)
    return values * half, half + 0.5 * values * (1.0 - tangent * tangent) * gelu_coef * (
        1.0 + 3.0 * 0.044715 * values * values
    )


def power_of_two(exponent):
    return jnp.where(
        exponent == -9,
        2.0**-9,
        jnp.where(exponent == -8, 2.0**-8, jnp.where(exponent == -7, 2.0**-7, 2.0**-6)),
    ).astype(F32)


def inverse_power(exponent):
    return jnp.where(
        exponent == -9,
        2.0**9,
        jnp.where(exponent == -8, 2.0**8, jnp.where(exponent == -7, 2.0**7, 2.0**6)),
    ).astype(F32)


def column_step(width):
    return 256 if width % 256 == 0 else width


def kernel(
    ndp,
    nz,
    x_hbm,
    c_hbm,
    e_hbm,
    wu_hbm,
    wd_hbm,
    so_ref,
    ig_ref,
    ug_ref,
    dg_ref,
    wu,
    wd,
    full,
    part,
    npart,
    ypart,
    zsum,
    zpart,
    shard,
    wide,
    acc,
    opart,
    odp,
    handed,
    turned,
    e_ref,
    w_sem,
    r_sem,
    e_sem,
    g_send,
    g_recv,
    n_send,
    n_recv,
    y_send,
    y_recv,
    z_send,
    z_recv,
    az_send,
    az_recv,
    an_recv,
    ay_send,
    ay_recv,
    o_send,
    o_recv,
    h_send,
    start_sem,
):
    sec = lax.axis_index("section")
    p = lax.axis_index("dp")
    q = lax.axis_index("tensor")
    y = q // nz
    z = q % nz
    micro = x_hbm.shape[0]
    tokens = ROWS * ndp
    half = wu.shape[2]
    cut = half // CUTS
    feats = wu.shape[1]
    my_dp = pl.ds(pl.multiple_of(p * ROWS, ROWS), ROWS)
    my_z = pl.ds(pl.multiple_of(z * ROWS, ROWS), ROWS)
    partner = {"tensor": (1 - y) * nz + z}

    def rows(index):
        return pl.ds(pl.multiple_of(index * ROWS, ROWS), ROWS)

    nx = ndp // NY

    def ring_order(n):
        return sorted(range(n), key=lambda offset: -min(offset, n - offset))

    dp_order = [(dx, dy) for dy in (1, 0) for dx in ring_order(nx)]
    z_order = ring_order(nz)
    near = sorted({1, nz - 1})
    far = [d for d in z_order if d not in near and d != 0]

    def dp_peer(j):
        dx, dy = dp_order[j]
        return lax.rem(p // NY + dx, nx) * NY + lax.rem(p + dy, NY)

    def z_peer(d):
        return y * nz + lax.rem(z + d, nz)

    def remote(src, dst, send, recv, where):
        pltpu.make_async_remote_copy(
            src_ref=src, dst_ref=dst, send_sem=send, recv_sem=recv, device_id=where, device_id_type=MESH
        ).start()

    def await_bytes(ref, sem):
        pltpu.make_async_copy(ref, ref, sem).wait()

    loads = []
    for h in range(NY):
        loads.append(pltpu.make_async_copy(wu_hbm.at[:, pl.ds(h * half, half)], wu.at[h], w_sem.at[0, h]))
        loads.append(pltpu.make_async_copy(wd_hbm.at[pl.ds(h * half, half)], wd.at[h], w_sem.at[1, h]))
    for load in loads:
        load.start()
    scales = pltpu.make_async_copy(e_hbm, e_ref, e_sem)
    scales.start()

    def own_rows(op):
        source = (x_hbm, c_hbm)[op]
        return [
            pltpu.make_async_copy(source.at[m], full.at[op, m, my_dp], r_sem.at[m]) for m in range(micro)
        ]

    for op in (XS, IS):

        @pl.when(sec == op)
        def _():
            for load in own_rows(op):
                load.start()

    barrier = pltpu.get_barrier_semaphore()

    for j in range(ndp):
        pl.semaphore_signal(
            barrier, inc=1, device_id={"section": 1 - sec, "dp": dp_peer(j)}, device_id_type=MESH
        )
    for j in range(ndp - 1):
        pl.semaphore_signal(barrier, inc=1, device_id={"dp": dp_peer(j)}, device_id_type=MESH)
    for d in z_order[:-1]:
        pl.semaphore_signal(barrier, inc=1, device_id={"tensor": z_peer(d)}, device_id_type=MESH)
    pl.semaphore_signal(barrier, inc=1, device_id=partner, device_id_type=MESH)
    pl.semaphore_wait(barrier, 2 * ndp + nz - 1)

    def gather_own(op):
        for m, load in enumerate(own_rows(op)):
            load.wait()
            mine = full.at[op, m, my_dp]

            for j in range(ndp - 1):
                remote(mine, mine, g_send.at[op, m], g_recv.at[op, m], {"dp": dp_peer(j)})

    def hand_over(op, m):
        for j in range(ndp):
            remote(
                handed.at[op, m],
                full.at[op, m, my_dp],
                h_send.at[op, m],
                g_recv.at[op, m],
                {"section": 1 - sec, "dp": dp_peer(j)},
            )

    def product(op, m, h, slot, c):
        step = column_step(cut)
        for j in range(cut // step):
            here = pl.ds(c * cut + j * step, step)
            if op == HID:
                value = jnp.dot(full[XS, m], wu[h, :, here], preferred_element_type=F32)
            else:
                value = lax.dot_general(
                    full[IS, m], wd[h, here, :], (((1,), (1,)), ((), ())), preferred_element_type=F32
                )
            part[op, m, slot, c, :, pl.ds(j * step, step)] = value.astype(BF)

    def there(d):
        return rows(lax.rem(z + d, nz))

    def stage_a(op, m, arrivals, before_sends=None):
        source = (XS, IS)[op]
        await_bytes(full.at[source, m, pl.ds(0, arrivals * ROWS)], g_recv.at[source, m])
        for c in range(CUTS):
            product(op, m, 1 - y, 0, c)
            if before_sends is not None and c == 0:
                before_sends()
            for k, d in enumerate(near):
                remote(
                    part.at[op, m, 0, c, there(d)],
                    npart.at[op, m, c, k],
                    n_send.at[op, m],
                    n_recv.at[op, m, c],
                    {"tensor": z_peer(d)},
                )
            for k, d in enumerate(far):
                remote(
                    part.at[op, m, 0, c, there(d)],
                    ypart.at[op, m, c, there(d)],
                    y_send.at[op, m],
                    y_recv.at[op, m, c, k],
                    partner,
                )
        for c in range(CUTS):
            product(op, m, y, 1, c)
            for k, d in enumerate(near):
                send_z(part.at[op, m, 1, c, there(d)], op, m, c, len(far) + k, d)

    def send_z(source, op, m, c, slot, d):
        remote(
            source,
            zpart.at[op, m, c, slot],
            z_send.at[op, m],
            z_recv.at[op, m, c],
            {"tensor": z_peer(d)},
        )

    def relay_near(op, m, c):
        await_bytes(npart.at[op, m, c], n_recv.at[op, m, c])
        total = part[op, m, 0, c, my_z, :].astype(F32)
        for k in range(len(near)):
            total = total + npart[op, m, c, k].astype(F32)
        zsum[op, m, c, my_z, :] = total.astype(BF)
        remote(
            zsum.at[op, m, c, my_z],
            ypart.at[op, m, c, my_z],
            y_send.at[op, m],
            y_recv.at[op, m, c, len(far)],
            partner,
        )

    def with_partner(op, m, c, k, d):
        piece = there(d)
        await_bytes(ypart.at[op, m, c, piece], y_recv.at[op, m, c, k])
        return part[op, m, 1, c, piece, :].astype(F32) + ypart[op, m, c, piece, :].astype(F32)

    def stage_b(op, m, c):
        for k, d in enumerate(far):
            if k == RELAY_AT:
                relay_near(op, m, c)
            zsum[op, m, c, there(d), :] = with_partner(op, m, c, k, d).astype(BF)
            send_z(zsum.at[op, m, c, there(d)], op, m, c, k, d)
        if RELAY_AT >= len(far):
            relay_near(op, m, c)

    def reduced(op, m, c):
        total = with_partner(op, m, c, len(far), 0)
        await_bytes(zpart.at[op, m, c], z_recv.at[op, m, c])
        for k in range(nz - 1):
            total = total + zpart[op, m, c, k].astype(F32)
        return total

    def spread(op, m, c, value):
        wide[op, m, y, c, my_z, :] = value
        mine = wide.at[op, m, y, c, my_z]
        for d in z_order[:-1]:
            remote(
                mine,
                mine,
                az_send.at[op, m],
                az_recv.at[op, m, c, z],
                {"tensor": z_peer(d)},
            )
        remote(mine, mine, ay_send.at[op, m], an_recv.at[op, m, c], partner)

    def stage_d(op, m, c):
        def arrived(d):
            piece = wide.at[op, m, y, c, there(d)]
            await_bytes(piece, az_recv.at[op, m, c, lax.rem(z + d, nz)])
            return piece

        opposite = wide.at[op, m, 1 - y, c, my_z]
        await_bytes(opposite, an_recv.at[op, m, c])
        for d in near:
            remote(opposite, opposite, ay_send.at[op, m], ay_recv.at[op, m], {"tensor": z_peer(d)})
        for d in far[::-1]:
            piece = arrived(d)
            remote(piece, piece, ay_send.at[op, m], ay_recv.at[op, m], partner)
        for d in near:
            arrived(d)

    def stage_e(op, m):
        def dots(h, finish):
            step = column_step(feats)
            for j in range(feats // step):
                at = pl.ds(j * step, step)
                value = None
                for c in range(CUTS):
                    here = pl.ds(c * cut, cut)
                    if op == OUT:
                        term = jnp.dot(wide[op, m, h, c], wd[h, here, at], preferred_element_type=F32)
                    else:
                        term = lax.dot_general(
                            wide[op, m, h, c],
                            wu[h, at, here],
                            (((1,), (1,)), ((), ())),
                            preferred_element_type=F32,
                        )
                    value = term if value is None else value + term
                finish(at, value)

        def first(at, value):
            acc[:, at] = value

        def second(at, value):
            opart[op, m, :, at] = (acc[:, at] + value).astype(BF)

        dots(y, first)
        await_bytes(wide.at[op, m, 1 - y, :, pl.ds(0, ROWS * (nz - 1))], ay_recv.at[op, m])
        dots(1 - y, second)

        for j in range(ndp - 1):
            to = dp_peer(j)
            remote(
                opart.at[op, m, rows(to)],
                odp.at[op, m, my_dp],
                o_send.at[op, m],
                o_recv.at[op, m],
                {"dp": to},
            )

        odp[op, m, my_dp, :] = opart[op, m, my_dp, :]

    def scattered(op, m):
        await_bytes(odp.at[op, m, pl.ds(0, ROWS * (ndp - 1))], o_recv.at[op, m])
        total = odp[op, m, pl.ds(0, ROWS), :].astype(F32)
        for k in range(1, ndp):
            total = total + odp[op, m, pl.ds(ROWS * k, ROWS), :].astype(F32)
        return total

    def finish_out(m):
        value = (full[XS, m, my_dp, :].astype(F32) + scattered(OUT, m)).astype(BF)
        so_ref[m] = value
        return value

    def finish_through(m):
        through = full[IS, m, my_dp, :].astype(F32) + scattered(THR, m)
        ig_ref[m] = through.astype(BF)
        return through

    def restore(m, through):
        for i in range(e_ref.shape[1]):
            for j in range(e_ref.shape[2]):
                tile = through[8 * i : 8 * i + 8, 128 * j : 128 * j + 128]
                exponent = e_ref[m, i, j]
                packed = jnp.clip(tile * inverse_power(exponent), -448.0, 448.0).astype(BF)
                acc[pl.ds(8 * i, 8), pl.ds(128 * j, 128)] = packed.astype(F32) * power_of_two(exponent)
        handed[IS, m] = acc[pl.ds(0, ROWS), :].astype(BF)

    def up_gradient():
        turned[...] = full[XS].reshape(micro * tokens, feats).T
        step = column_step(cut)
        for h in range(NY):
            for c in range(CUTS):
                for j in range(cut // step):
                    right = wide[DEL, :, h, c, :, pl.ds(j * step, step)].reshape(micro * tokens, step)
                    ug_ref[:, pl.ds(h * half + c * cut + j * step, step)] = jnp.dot(
                        turned[...], right, preferred_element_type=F32
                    ).astype(BF)

    def down_gradient():
        step = column_step(cut)
        for h in range(NY):
            for c in range(CUTS):
                for j in range(cut // step):
                    left = wide[ACT, :, h, c, :, pl.ds(j * step, step)].reshape(micro * tokens, step)
                    dg_ref[pl.ds(h * half + c * cut + j * step, step), :] = lax.dot_general(
                        left,
                        full[IS].reshape(micro * tokens, feats),
                        (((0,), (0,)), ((), ())),
                        preferred_element_type=F32,
                    ).astype(BF)

    def all_of(stage, *args):
        for m in range(micro):
            stage(*args, m)

    def all_cuts(stage, *args):
        for m in range(micro):
            for c in range(CUTS):
                stage(*args, m, c)

    def strip(c):
        return pl.ds(c * cut, cut)

    @pl.when(sec == 0)
    def _():
        gather_own(XS)
        for load in loads:
            load.wait()
        scales.wait()

        def forward_c(m, c):
            active, slope = gelu_parts(reduced(HID, m, c))
            spread(ACT, m, c, active.astype(BF))
            shard[HID, m, :, strip(c)] = slope

        def forward_f(m):
            handed[XS, m] = finish_out(m)
            hand_over(XS, m)

        def backward_c(m, c):
            spread(DEL, m, c, (reduced(BACK, m, c) * shard[HID, m, :, strip(c)]).astype(BF))

        for m in range(micro):
            stage_a(HID, m, ndp - 1)
        all_cuts(stage_b, HID)
        all_cuts(forward_c)
        all_cuts(stage_d, ACT)
        pl.semaphore_signal(start_sem, inc=1, device_id={"section": 1}, device_id_type=MESH)
        all_of(stage_e, OUT)
        all_of(forward_f)

        for m in range(micro):
            stage_a(BACK, m, ndp)
        all_cuts(stage_b, BACK)
        down_gradient()
        all_cuts(backward_c)
        all_cuts(stage_d, DEL)
        all_of(stage_e, THR)
        up_gradient()
        all_of(finish_through)

    @pl.when(sec == 1)
    def _():
        gather_own(IS)
        for load in loads:
            load.wait()
        scales.wait()

        def wait_start():
            pl.semaphore_wait(start_sem, 1)

        def early_c(m, c):
            shard[BACK, m, :, strip(c)] = reduced(BACK, m, c)

        def turn_c(m, c):
            active, slope = gelu_parts(reduced(HID, m, c))
            spread(DEL, m, c, (shard[BACK, m, :, strip(c)] * slope).astype(BF))
            shard[HID, m, :, strip(c)] = active

        def turn_f(m):
            restore(m, finish_through(m))
            hand_over(IS, m)

        def late_c(m, c):
            spread(ACT, m, c, shard[HID, m, :, strip(c)].astype(BF))

        for m in range(micro):
            stage_a(BACK, m, ndp - 1, wait_start if m == 0 else None)
        all_cuts(stage_b, BACK)
        all_cuts(early_c)

        for m in range(micro):
            stage_a(HID, m, ndp)
        all_cuts(stage_b, HID)
        all_cuts(turn_c)
        all_cuts(stage_d, DEL)
        all_of(stage_e, THR)
        all_of(turn_f)

        for m in range(micro):
            for c in range(CUTS):
                late_c(m, c)
                if m == 0 and c == 0:
                    up_gradient()
                stage_d(ACT, m, c)
        all_of(stage_e, OUT)
        down_gradient()
        all_of(finish_out)

    for m in range(micro):
        for op in range(2):
            await_bytes(part.at[op, m, 0, :, pl.ds(0, ROWS * (len(far) + 1))], y_send.at[op, m])
            await_bytes(part.at[op, m, 0, :, pl.ds(0, ROWS * len(near))], n_send.at[op, m])
            await_bytes(zsum.at[op, m, :, pl.ds(0, ROWS * (nz - 1))], z_send.at[op, m])
            await_bytes(wide.at[op, m, 0, :, pl.ds(0, ROWS * (nz - 1))], az_send.at[op, m])
            await_bytes(wide.at[op, m, 0], ay_send.at[op, m])
            await_bytes(opart.at[op, m, pl.ds(0, ROWS * (ndp - 1))], o_send.at[op, m])

        @pl.when(sec == 0)
        def _():
            await_bytes(full.at[XS, m, pl.ds(0, ROWS * (ndp - 1))], g_send.at[XS, m])
            await_bytes(full.at[XS, m], h_send.at[XS, m])

        @pl.when(sec == 1)
        def _():
            await_bytes(full.at[IS, m, pl.ds(0, ROWS * (ndp - 1))], g_send.at[IS, m])
            await_bytes(full.at[IS, m], h_send.at[IS, m])


def flush(*refs):
    arrays = len(refs) // 2
    sems = refs[-1]
    copies = [
        pltpu.make_async_copy(refs[i], refs[arrays + i], sems.at[i]) for i in range(arrays)
    ]
    for copy in copies:
        copy.start()
    for copy in copies:
        copy.wait()


def per_device(ndp, ntensor, inputs, cotangent, scale_exps, up_weight, down_weight):
    nz = ntensor // NY
    micro, own_rows, feats = inputs.shape
    units = up_weight.shape[2]
    half = units // NY
    cut = half // CUTS
    tokens = own_rows * ndp
    vmem = pl.BlockSpec(memory_space=pltpu.VMEM)
    far = pl.BlockSpec(memory_space=pltpu.HBM)
    dma = pltpu.SemaphoreType.DMA
    results = pl.pallas_call(
        functools.partial(kernel, ndp, nz),
        out_shape=[
            jax.ShapeDtypeStruct(inputs.shape, BF),
            jax.ShapeDtypeStruct(inputs.shape, BF),
            jax.ShapeDtypeStruct((feats, units), BF),
            jax.ShapeDtypeStruct((units, feats), BF),
        ],
        in_specs=[far] * 5,
        out_specs=[vmem] * 4,
        scratch_shapes=[
            pltpu.VMEM((NY, feats, half), BF),
            pltpu.VMEM((NY, half, feats), BF),
            pltpu.VMEM((2, micro, tokens, feats), BF),
            pltpu.VMEM((2, micro, 2, CUTS, tokens, cut), BF),
            pltpu.VMEM((2, micro, CUTS, len({1, nz - 1}), ROWS, cut), BF),
            pltpu.VMEM((2, micro, CUTS, tokens, cut), BF),
            pltpu.VMEM((2, micro, CUTS, tokens, cut), BF),
            pltpu.VMEM((2, micro, CUTS, nz - 1, ROWS, cut), BF),
            pltpu.VMEM((2, micro, ROWS, half), F32),
            pltpu.VMEM((2, micro, NY, CUTS, tokens, cut), BF),
            pltpu.VMEM((tokens, feats), F32),
            pltpu.VMEM((2, micro, tokens, feats), BF),
            pltpu.VMEM((2, micro, tokens, feats), BF),
            pltpu.VMEM((2, micro, ROWS, feats), BF),
            pltpu.VMEM((feats, micro * tokens), BF),
            pltpu.SMEM(scale_exps.shape, jnp.int32),
            dma((2, NY)),
            dma((micro,)),
            dma,
            dma((2, micro)),
            dma((2, micro)),
            dma((2, micro)),
            dma((2, micro, CUTS)),
            dma((2, micro)),
            dma((2, micro, CUTS, nz)),
            dma((2, micro)),
            dma((2, micro, CUTS)),
            dma((2, micro)),
            dma((2, micro, CUTS, nz)),
            dma((2, micro, CUTS)),
            dma((2, micro)),
            dma((2, micro)),
            dma((2, micro)),
            dma((2, micro)),
            dma((2, micro)),
            pltpu.SemaphoreType.REGULAR,
        ],
        compiler_params=pltpu.CompilerParams(
            collective_id=0, has_side_effects=True, vmem_limit_bytes=48 * 1024 * 1024
        ),
        name="relay",
    )(*[pltpu.with_memory_space_constraint(a, pltpu.HBM) for a in (inputs, cotangent, scale_exps, up_weight[0], down_weight[0])])
    section_out, input_grads, up_grads, down_grads = pl.pallas_call(
        flush,
        out_shape=[jax.ShapeDtypeStruct(result.shape, result.dtype) for result in results],
        in_specs=[vmem] * 4,
        out_specs=[pl.BlockSpec(memory_space=pl.ANY)] * 4,
        scratch_shapes=[dma((4,))],
        compiler_params=pltpu.CompilerParams(vmem_limit_bytes=1024 * 1024),
        name="flush",
    )(*[pltpu.with_memory_space_constraint(result, pltpu.VMEM) for result in results])
    return section_out[None], input_grads[None], up_grads[None], down_grads[None]


def solution(mesh):
    in_specs = (
        P(None, "dp", "tensor"),
        P(None, "dp", "tensor"),
        P(None, "dp", "tensor"),
        P("section", "tensor", "dp"),
        P("section", "dp", "tensor"),
    )
    out_specs = (
        P("section", None, "dp", "tensor"),
        P("section", None, "dp", "tensor"),
        P("section", "tensor", "dp"),
        P("section", "dp", "tensor"),
    )
    return jax.shard_map(
        functools.partial(per_device, mesh.shape["dp"], mesh.shape["tensor"]),
        mesh=mesh,
        in_specs=in_specs,
        out_specs=out_specs,
        check_vma=False,
    )
```

time: 122 us -> 115 us (0.943)
  Pallas kernels: 121 us -> 114 us
    pallas_call x1, Pallas kernels: 119 us -> 111 us  [per_device(): pl.pallas_call(functools.partial(kernel, ndp, nz), out_shape=[jax.ShapeDt...]
where the time goes in v3:
time: 115 us
  Pallas kernels  114 us (99%)
    pallas_call x1, Pallas kernels, per_device(): pl.pallas_call(functools.partial(kernel, ndp, nz), out_shape=[jax.ShapeDt...  111 us
    pallas_call x1, Pallas kernels, per_device(): pl.pallas_call(flush, out_shape=[jax.ShapeDtypeStruct(result.shape, resul...  2.41 us

profile of v3, /device:TPU:2, one launch (start us, length us, event | category | flops | bytes accessed | tf_op | source)
XLA Modules:
  0.0 114.7 jit_solution(17384249464753568497)
XLA Ops:
  0.6 111.5 %relay.1 = (bf16[2,16,512]{2,1,0:T(8,128)(2,1)S(1)}, bf16[2,16,512]{2,1,0:T(8,128)(2,1)S(1)}, bf16[512,2560]{1,0:T(8,128)(2,1)S(1)}, bf16[2560,512]{1,0:T(8,128)(2,1)S(1)}) custom-call(bf16[2,16,512]{2,1,0:T(8,128)(2,1)} %x_hbm.1, bf16[2,16,512]{2,1,0:T(8,128)(2,1)} %c_hbm.1, s32[2,2,4]{2,1,0:T(2,128)} %e_hbm.1, bf16[512,2560]{1,0:T(8,128)(2,1)} %bitcast.6, ...), custom_call_target="tpu_custom_call" | custom-call | tf_op jit(solution)/shard_map/relay/pallas_call | solution.py:548
  112.1 2.4 %flush.1 = (bf16[2,16,512]{2,1,0:T(8,128)(2,1)}, bf16[2,16,512]{2,1,0:T(8,128)(2,1)}, bf16[512,2560]{1,0:T(8,128)(2,1)}, bf16[2560,512]{1,0:T(8,128)(2,1)}) custom-call(bf16[2,16,512]{2,1,0:T(8,128)(2,1)S(1)} %get-tuple-element.12.refs_0_, bf16[2,16,512]{2,1,0:T(8,128)(2,1)S(1)} %get-tuple-element.13.refs_1_, ...), custom_call_target="tpu_custom_call" | custom-call | tf_op jit(solution)/shard_map/flush/pallas_call | solution.py:601

commit v4 on v3

--- a/solution.py
+++ b/solution.py
@@ -448,6 +448,7 @@
         for m in range(micro):
             stage_a(BACK, m, ndp)
         all_cuts(stage_b, BACK)
+        pl.semaphore_signal(start_sem, inc=1, device_id={"section": 1}, device_id_type=MESH)
         down_gradient()
         all_cuts(backward_c)
         all_cuts(stage_d, DEL)
@@ -490,14 +491,15 @@
         all_cuts(stage_b, HID)
         all_cuts(turn_c)
         all_cuts(stage_d, DEL)
+        all_cuts(late_c)
         all_of(stage_e, THR)
         all_of(turn_f)
 
+        up_gradient()
         for m in range(micro):
+            if m == micro - 1:
+                wait_start()
             for c in range(CUTS):
-                late_c(m, c)
-                if m == 0 and c == 0:
-                    up_gradient()
                 stage_d(ACT, m, c)
         all_of(stage_e, OUT)
         down_gradient()

time: 115 us -> 111 us (0.965)
  Pallas kernels: 114 us -> 110 us
    pallas_call x1, Pallas kernels: 111 us -> 108 us  [per_device(): pl.pallas_call(functools.partial(kernel, ndp, nz), out_shape=[jax.ShapeDt...]
where the time goes in v4:
time: 111 us
  Pallas kernels  110 us (99%)
    pallas_call x1, Pallas kernels, per_device(): pl.pallas_call(functools.partial(kernel, ndp, nz), out_shape=[jax.ShapeDt...  108 us
    pallas_call x1, Pallas kernels, per_device(): pl.pallas_call(flush, out_shape=[jax.ShapeDtypeStruct(result.shape, resul...  2.41 us

profile of v4, /device:TPU:2, one launch (start us, length us, event | category | flops | bytes accessed | tf_op | source)
XLA Modules:
  0.0 111.2 jit_solution(12133504731825282523)
XLA Ops:
  0.6 108.0 %relay.1 = (bf16[2,16,512]{2,1,0:T(8,128)(2,1)S(1)}, bf16[2,16,512]{2,1,0:T(8,128)(2,1)S(1)}, bf16[512,2560]{1,0:T(8,128)(2,1)S(1)}, bf16[2560,512]{1,0:T(8,128)(2,1)S(1)}) custom-call(bf16[2,16,512]{2,1,0:T(8,128)(2,1)} %x_hbm.1, bf16[2,16,512]{2,1,0:T(8,128)(2,1)} %c_hbm.1, s32[2,2,4]{2,1,0:T(2,128)} %e_hbm.1, bf16[512,2560]{1,0:T(8,128)(2,1)} %bitcast.6, ...), custom_call_target="tpu_custom_call" | custom-call | tf_op jit(solution)/shard_map/relay/pallas_call | solution.py:550
  108.7 2.4 %flush.1 = (bf16[2,16,512]{2,1,0:T(8,128)(2,1)}, bf16[2,16,512]{2,1,0:T(8,128)(2,1)}, bf16[512,2560]{1,0:T(8,128)(2,1)}, bf16[2560,512]{1,0:T(8,128)(2,1)}) custom-call(bf16[2,16,512]{2,1,0:T(8,128)(2,1)S(1)} %get-tuple-element.12.refs_0_, bf16[2,16,512]{2,1,0:T(8,128)(2,1)S(1)} %get-tuple-element.13.refs_1_, ...), custom_call_target="tpu_custom_call" | custom-call | tf_op jit(solution)/shard_map/flush/pallas_call | solution.py:603
